TPU v7x, 32 devices: a whole 2x2x4 slice. The times are simulated.
32 devices in a mesh: fsdp: 32 (over z, y, x, core).
Axes of the slice: x: 2, y: 2, z: 4, core: 2. Of those that a mesh axis runs over, the one named last changes fastest.
Arguments:
- tokens: bfloat16 [4096, 768], P('fsdp')
- doc_ids: int32 [4096], P('fsdp'), may hold values from 0 to 3, as said below
- pad_mask: int32 [4096], P('fsdp'), may hold values from 0 to 1, as said below
- qkv_matrix: bfloat16 [768, 2304], P('fsdp'), may hold values from -0.21875 to 0.21875
- query_bias: bfloat16 [768], P('fsdp'), may hold values from -3 to 3
- value_bias: bfloat16 [768], P('fsdp'), may hold values from -3 to 3
- out_matrix: bfloat16 [768, 768], P('fsdp'), may hold values from -1.75 to 1.75
- out_bias: bfloat16 [768], P('fsdp'), may hold values from -3 to 3
- attn_gain: bfloat16 [768], P('fsdp'), may hold values from 0.25 to 1.75
- attn_shift: bfloat16 [768], P('fsdp'), may hold values from -3 to 3
- up_matrix: bfloat16 [768, 3072], P('fsdp'), may hold values from -0.21875 to 0.21875
- up_bias: bfloat16 [3072], P('fsdp'), may hold values from -3 to 3
- down_matrix: bfloat16 [3072, 768], P('fsdp'), may hold values from -0.109375 to 0.109375
- down_bias: bfloat16 [768], P('fsdp'), may hold values from -3 to 3
- ffn_gain: bfloat16 [768], P('fsdp'), may hold values from 0.25 to 1.75
- ffn_shift: bfloat16 [768], P('fsdp'), may hold values from -3 to 3
- cotangent: bfloat16 [4096, 768], P('fsdp'), may hold values from -6 to 6
Outputs:
- layer_out: bfloat16 [4096, 768], P('fsdp')
- token_grad: float32 [4096, 768], P('fsdp')
- grad_qkv: float32 [768, 2304], P('fsdp')
- grad_qbias: float32 [768], P('fsdp')
- grad_vbias: float32 [768], P('fsdp')
- grad_outmat: float32 [768, 768], P('fsdp')
- grad_outbias: float32 [768], P('fsdp')
- grad_gain_one: float32 [768], P('fsdp')
- grad_shift_one: float32 [768], P('fsdp')
- grad_upmat: float32 [768, 3072], P('fsdp')
- grad_upbias: float32 [3072], P('fsdp')
- grad_downmat: float32 [3072, 768], P('fsdp')
- grad_downbias: float32 [768], P('fsdp')
- grad_gain_two: float32 [768], P('fsdp')
- grad_shift_two: float32 [768], P('fsdp')
Inputs may be any that keep to these rules, and one draw needn't show every extreme that they name: `doc_ids`: within each block of 128 rows the ids never fall; the first row has 0 and the last 3; rows with one id are one sequence, padding continues the last one. `pad_mask`: within each block of 128 rows the ones come first and number from 32 to 128; some block is all ones and some has exactly 32.
All inputs are finite; a program needn't handle non-finite values.
Results may differ from a plain program's by a relative error of at most 0.01.
Values may be sent and summed in bfloat16 or wider, within the bound.
A program may use at most 192 MiB of HBM per device.

v0:
```python
import functools
import math

import jax
import jax.numpy as jnp
from jax import lax
from jax.experimental import pallas as pl
from jax.experimental.pallas import tpu as pltpu
from jax.sharding import PartitionSpec as P

HEADS = 12
AXIS = "fsdp"
MESH_IDS = pl.DeviceIdType.MESH
BITS = 5
GROUP = 32
CORE, X, Y, Z1, Z2 = 0, 1, 2, 3, 4
SCATTER_ORDERS = (
    (CORE, X, Y, Z1, Z2),
    (CORE, X, Y, Z1, Z2),
    (CORE, Y, X, Z1, Z2),
    (CORE, Z1, Z2, X, Y),
    (CORE, Z1, Z2, X, Y),
)
VMEM_BYTES = 60 * 1024 * 1024


def bits_of(me):
    return [lax.rem(lax.div(me, 1 << b), 2) for b in range(BITS)]


def toggled(me, mine, r):
    for b in range(BITS):
        if r >> b & 1:
            me = me + (1 << b) * (1 - 2 * mine[b])
    return me


def greet(me, mine):
    barrier = pltpu.get_barrier_semaphore()
    for b in range(BITS):
        pl.semaphore_signal(
            barrier, inc=1, device_id=(toggled(me, mine, 1 << b),), device_id_type=MESH_IDS
        )
    pl.semaphore_wait(barrier, BITS)


def gather_kernel(count, *refs):
    shards, wholes = refs[:count], refs[count : 2 * count]
    send_sem, recv_sem, local_sem = refs[2 * count :]
    me = lax.axis_index(AXIS)
    mine = bits_of(me)
    greet(me, mine)

    def move(k, r, b):
        owner = toggled(me, mine, r)
        source = shards[k] if r == 0 else wholes[k].at[owner]
        slot = r | (1 << b)
        return pltpu.make_async_remote_copy(
            src_ref=source,
            dst_ref=wholes[k].at[owner],
            send_sem=send_sem.at[k, slot],
            recv_sem=recv_sem.at[k, slot],
            device_id=(toggled(me, mine, 1 << b),),
            device_id_type=MESH_IDS,
        )

    def landed(k, r):
        here = wholes[k].at[toggled(me, mine, r)]
        pltpu.make_async_remote_copy(
            src_ref=here,
            dst_ref=here,
            send_sem=send_sem.at[k, r],
            recv_sem=recv_sem.at[k, r],
            device_id=(toggled(me, mine, 1),),
            device_id_type=MESH_IDS,
        ).wait_recv()

    orders = [tuple(reversed(SCATTER_ORDERS[k])) for k in range(count)]
    own = [
        pltpu.make_async_copy(shards[k], wholes[k].at[me], local_sem.at[k]) for k in range(count)
    ]
    sent = [[] for _ in range(count)]
    for k in range(count):
        for b in orders[k]:
            copy = move(k, 0, b)
            copy.start()
            sent[k].append(copy)
    for copy in own:
        copy.start()
    have = [[0] for _ in range(count)]
    for step in range(BITS):
        width = 1 << step
        for i in range(width):
            for k in range(count):
                b = orders[k][step]
                r = have[k][i] | (1 << b)
                landed(k, r)
                for later in orders[k][step + 1 :]:
                    copy = move(k, r, later)
                    copy.start()
                    sent[k].append(copy)
        for k in range(count):
            b = orders[k][step]
            have[k] = have[k] + [r | (1 << b) for r in have[k]]
    for k in range(count):
        own[k].wait()
        for copy in sent[k]:
            copy.wait_send()


def gather_all(shards):
    count = len(shards)
    return pl.pallas_call(
        functools.partial(gather_kernel, count),
        out_shape=[jax.ShapeDtypeStruct((GROUP,) + s.shape, s.dtype) for s in shards],
        in_specs=[pl.BlockSpec(memory_space=pl.ANY)] * count,
        out_specs=[pl.BlockSpec(memory_space=pl.ANY)] * count,
        scratch_shapes=[
            pltpu.SemaphoreType.DMA((count, GROUP)),
            pltpu.SemaphoreType.DMA((count, GROUP)),
            pltpu.SemaphoreType.DMA((count,)),
        ],
        compiler_params=pltpu.CompilerParams(collective_id=0, has_side_effects=True),
        name="gather_all",
    )(*shards)


def priority(order, step):
    left = order[step + 1 :]
    blocks = [0]
    for b in reversed(left):
        blocks = [r | (1 << b) for r in blocks] + blocks
    return blocks


def scatter_kernel(count, *refs):
    parts, outs = refs[:count], refs[count : 2 * count]
    landing = refs[2 * count : 3 * count]
    send_sem, recv_sem = refs[3 * count :]
    me = lax.axis_index(AXIS)
    mine = bits_of(me)
    greet(me, mine)

    slot_of = []
    for k in range(count):
        table, used = {}, 0
        for step in range(BITS):
            for r in priority(SCATTER_ORDERS[k], step):
                table[step, r] = used
                used += 1
        slot_of.append(table)

    def held(k, step, r):
        if step < 0:
            return parts[k].at[toggled(me, mine, r)]
        return landing[k].at[slot_of[k][step, r]]

    def move(k, step, r):
        b = SCATTER_ORDERS[k][step]
        slot = slot_of[k][step, r & ~(1 << b)]
        return pltpu.make_async_remote_copy(
            src_ref=held(k, step - 1, r),
            dst_ref=landing[k].at[slot],
            send_sem=send_sem.at[k, slot],
            recv_sem=recv_sem.at[k, slot],
            device_id=(toggled(me, mine, 1 << b),),
            device_id_type=MESH_IDS,
        )

    copies = {}
    for i in range(GROUP // 2):
        for k in range(count):
            order = SCATTER_ORDERS[k]
            r = priority(order, 0)[i]
            copy = move(k, 0, r | (1 << order[0]))
            copy.start()
            copies[k, 0, r] = copy
    for step in range(BITS):
        for i in range(1 << (BITS - 1 - step)):
            for k in range(count):
                order = SCATTER_ORDERS[k]
                r = priority(order, step)[i]
                copies[k, step, r].wait_recv()
                before, now = held(k, step - 1, r), held(k, step, r)
                columns = now.shape[-1]
                last = step == BITS - 1
                tile = min(columns, 768 if now.shape[0] <= 24 else 256)

                def add(j, carry, before=before, now=now, tile=tile, last=last, k=k):
                    at = pl.ds(pl.multiple_of(j * tile, tile), tile)
                    total = now[:, at].astype(jnp.float32) + before[:, at].astype(jnp.float32)
                    if last:
                        outs[k][:, at] = total
                    else:
                        now[:, at] = total.astype(jnp.bfloat16)
                    return carry

                lax.fori_loop(0, columns // tile, add, 0)
                if not last and r >> order[step + 1] & 1:
                    copy = move(k, step + 1, r)
                    copy.start()
                    copies[k, step + 1, r & ~(1 << order[step + 1])] = copy
    for copy in copies.values():
        copy.wait_send()


def scatter_all(parts):
    count = len(parts)
    return pl.pallas_call(
        functools.partial(scatter_kernel, count),
        out_shape=[jax.ShapeDtypeStruct(p.shape[1:], jnp.float32) for p in parts],
        in_specs=[pl.BlockSpec(memory_space=pltpu.VMEM)] * count,
        out_specs=[pl.BlockSpec(memory_space=pltpu.VMEM)] * count,
        scratch_shapes=[pltpu.VMEM((GROUP - 1,) + p.shape[1:], p.dtype) for p in parts]
        + [
            pltpu.SemaphoreType.DMA((count, GROUP)),
            pltpu.SemaphoreType.DMA((count, GROUP)),
        ],
        compiler_params=pltpu.CompilerParams(
            collective_id=1, has_side_effects=True, vmem_limit_bytes=VMEM_BYTES
        ),
        name="scatter_all",
    )(*parts)


norm_eps = 1e-06
root_half = 0.7071067811865476
inv_root_two_pi = 0.3989422804014327


def layer_norm(values, gain, shift):
    centred = values - jnp.mean(values, axis=-1, keepdims=True)
    inverse = lax.rsqrt(jnp.mean(centred * centred, axis=-1, keepdims=True) + norm_eps)
    normed = centred * inverse
    return (normed * gain + shift, normed, inverse)


def norm_back(upstream, normed, inverse, gain):
    scaled = upstream * gain
    return inverse * (
        scaled
        - jnp.mean(scaled, axis=-1, keepdims=True)
        - normed * jnp.mean(scaled * normed, axis=-1, keepdims=True)
    )


def masked_scores(query, key_rows, visible, score_scale):
    scores = (
        jnp.einsum("qhd,khd->hqk", query, key_rows, preferred_element_type=jnp.float32)
        * score_scale
    )
    return jnp.where(visible[None], scores, -1e30)


def vector_rows(vectors):
    rows = [jnp.pad(v, ((0, 0), (0, 128 - v.shape[1]))) for v in vectors]
    rows = rows + [jnp.zeros_like(rows[0])] * (16 - len(rows))
    return jnp.stack(rows, axis=1)


def attention_back_kernel(
    scale, qkv_ref, back_ref, doc_col, doc_row, pad_row, d_qkv_ref, sums_ref
):
    fl = jnp.float32
    rows, width = back_ref.shape
    size = width // HEADS
    across, down, both = ((1,), (0,)), ((0,), (0,)), ((1,), (1,))

    def dot(a, b, over):
        return lax.dot_general(a, b, (over, ((), ())), preferred_element_type=fl)

    square = (rows, rows)
    same = lax.broadcasted_iota(jnp.int32, square, 0) == lax.broadcasted_iota(
        jnp.int32, square, 1
    )
    visible = (doc_col[...] == doc_row[...]) & ((pad_row[...] == 1) | same)
    for pair in range(HEADS // 2):
        results = []
        for h in (2 * pair, 2 * pair + 1):
            query, key_rows, value_rows = (
                qkv_ref[:, part * width + h * size : part * width + (h + 1) * size]
                for part in range(3)
            )
            back = back_ref[:, h * size : (h + 1) * size]
            scores = jnp.where(visible, dot(query, key_rows, both) * scale, -1e30)
            row_max = jnp.max(scores, axis=-1, keepdims=True)
            total = jnp.sum(jnp.exp(scores - row_max), axis=-1, keepdims=True)
            probs = jnp.exp(scores - (row_max + jnp.log(total)))
            d_value = dot(probs.astype(jnp.bfloat16), back, down)
            d_probs = dot(back, value_rows, both)
            delta = jnp.sum(probs * d_probs, axis=-1, keepdims=True)
            d_scores = (probs * (d_probs - delta) * scale).astype(jnp.bfloat16)
            results.append(
                (dot(d_scores, key_rows, across), dot(d_scores, query, down), d_value)
            )
        for part in range(3):
            block = jnp.concatenate([results[0][part], results[1][part]], axis=1)
            at = pair * 2 * size
            d_qkv_ref[:, part * width + at : part * width + at + 2 * size] = block.astype(
                jnp.bfloat16
            )
            if part != 1:
                row = part // 2
                sums_ref[row : row + 1, at : at + 2 * size] = jnp.sum(
                    block, axis=0, keepdims=True
                )


def attention_back(qkv, d_context, doc_ids, pad_mask):
    rows, width = d_context.shape
    return pl.pallas_call(
        functools.partial(attention_back_kernel, 1.0 / math.sqrt(width // HEADS)),
        out_shape=(
            jax.ShapeDtypeStruct(qkv.shape, jnp.bfloat16),
            jax.ShapeDtypeStruct((2, width), jnp.float32),
        ),
        compiler_params=pltpu.CompilerParams(vmem_limit_bytes=24 * 1024 * 1024),
        name="attention_back",
    )(qkv, d_context, doc_ids[:, None], doc_ids[None], pad_mask[None])


def grad_rows(left, right):
    return jnp.einsum("ra,rb->ab", left, right, preferred_element_type=jnp.float32)


def local(
    tokens,
    doc_ids,
    pad_mask,
    qkv_matrix,
    query_bias,
    value_bias,
    out_matrix,
    out_bias,
    attn_gain,
    attn_shift,
    up_matrix,
    up_bias,
    down_matrix,
    down_bias,
    ffn_gain,
    ffn_shift,
    cotangent,
):
    fl = jnp.float32
    in_kernels = lax.axis_size(AXIS) == GROUP
    owned_vectors = (
        query_bias,
        value_bias,
        out_bias,
        attn_gain,
        attn_shift,
        down_bias,
        ffn_gain,
        ffn_shift,
        up_bias,
    )
    vectors = vector_rows([v[None] for v in owned_vectors])[0]
    if in_kernels:
        wholes = gather_all([qkv_matrix, out_matrix, up_matrix, down_matrix, vectors])
        wholes = [w.reshape((-1, w.shape[-1])) for w in wholes]
    else:
        wholes = [
            lax.all_gather(w, AXIS, axis=0, tiled=True)
            for w in (qkv_matrix, out_matrix, up_matrix, down_matrix, vectors)
        ]
    qkv_full, outm_full, upm_full, downm_full, vectors_full = wholes
    vectors_full = vectors_full.reshape((-1,) + vectors.shape)
    (
        qbias_full,
        vbias_full,
        outb_full,
        gain_one,
        shift_one,
        downb_full,
        gain_two,
        shift_two,
        upb_full,
    ) = (vectors_full[:, j, : v.shape[0]].reshape(-1) for j, v in enumerate(owned_vectors))
    qkv_back, outm_back, upm_back, downm_back = qkv_full, outm_full, upm_full, downm_full
    gain_one_back, gain_two_back = gain_one, gain_two
    row_count, model_width = tokens.shape
    head_size = model_width // HEADS
    score_scale = 1.0 / math.sqrt(head_size)
    hidden_width = upm_full.shape[1]
    ratio = hidden_width // model_width
    zero_part = jnp.zeros((model_width,), fl)
    qkv = jnp.dot(tokens, qkv_full, preferred_element_type=fl)
    qkv = (qkv + jnp.concatenate([qbias_full.astype(fl), zero_part, vbias_full.astype(fl)])).astype(
        jnp.bfloat16
    )
    query = qkv[:, :model_width].reshape(row_count, HEADS, head_size)
    key_rows = qkv[:, model_width : 2 * model_width].reshape(row_count, HEADS, head_size)
    value_rows = qkv[:, 2 * model_width :].reshape(row_count, HEADS, head_size)
    positions = jnp.arange(row_count)
    visible = (doc_ids[:, None] == doc_ids[None, :]) & (
        (pad_mask[None, :] == 1) | (positions[:, None] == positions[None, :])
    )
    scores = masked_scores(query, key_rows, visible, score_scale)
    row_max = jnp.max(scores, axis=-1, keepdims=True)
    log_total = row_max + jnp.log(jnp.sum(jnp.exp(scores - row_max), axis=-1, keepdims=True))
    probs_b = jnp.exp(scores - log_total).astype(jnp.bfloat16)
    context = jnp.einsum("hqk,khd->qhd", probs_b, value_rows, preferred_element_type=fl)
    context = context.reshape(row_count, model_width).astype(jnp.bfloat16)
    attn_sum = (
        tokens.astype(fl)
        + jnp.dot(context, outm_full, preferred_element_type=fl)
        + outb_full.astype(fl)
    )
    hidden, normed_one, inverse_one = layer_norm(
        attn_sum, gain_one.astype(fl), shift_one.astype(fl)
    )
    hidden_b = hidden.astype(jnp.bfloat16)
    pre_act = jnp.dot(hidden_b, upm_full, preferred_element_type=fl) + upb_full.astype(fl)
    cdf_part = 0.5 * (1.0 + jax.scipy.special.erf(pre_act * root_half))
    pdf_part = jnp.exp(-0.5 * pre_act * pre_act) * inv_root_two_pi
    activation = (pre_act * cdf_part).astype(jnp.bfloat16)
    ffn_sum = (
        hidden + jnp.dot(activation, downm_full, preferred_element_type=fl) + downb_full.astype(fl)
    )
    normed_out, normed_two, inverse_two = layer_norm(
        ffn_sum, gain_two.astype(fl), shift_two.astype(fl)
    )
    layer_out = normed_out.astype(jnp.bfloat16)
    upstream = cotangent.astype(fl)
    g_gain_two = jnp.sum(upstream * normed_two, axis=0)
    g_shift_two = jnp.sum(upstream, axis=0)
    d_ffn = norm_back(upstream, normed_two, inverse_two, gain_two_back.astype(fl))
    g_down_b = jnp.sum(d_ffn, axis=0)
    d_ffn_b = d_ffn.astype(jnp.bfloat16)
    d_act = jnp.einsum("rd,fd->rf", d_ffn_b, downm_back, preferred_element_type=fl)
    d_pre = d_act * (cdf_part + pre_act * pdf_part)
    g_up_b = jnp.sum(d_pre, axis=0)
    d_pre_b = d_pre.astype(jnp.bfloat16)
    d_hidden = d_ffn + jnp.einsum("rf,df->rd", d_pre_b, upm_back, preferred_element_type=fl)
    g_gain_one = jnp.sum(d_hidden * normed_one, axis=0)
    g_shift_one = jnp.sum(d_hidden, axis=0)
    d_attn = norm_back(d_hidden, normed_one, inverse_one, gain_one_back.astype(fl))
    g_out_b = jnp.sum(d_attn, axis=0)
    d_attn_b = d_attn.astype(jnp.bfloat16)
    d_context = jnp.einsum("re,de->rd", d_attn_b, outm_back, preferred_element_type=fl).astype(
        jnp.bfloat16
    )
    d_qkv, attn_sums = attention_back(qkv, d_context, doc_ids, pad_mask)
    g_qbias, g_vbias = attn_sums[0], attn_sums[1]
    token_grad = d_attn + jnp.einsum("re,de->rd", d_qkv, qkv_back, preferred_element_type=fl)
    sums = vector_rows(
        [
            g.reshape((lax.axis_size(AXIS), -1))
            for g in (
                g_qbias,
                g_vbias,
                g_out_b,
                g_gain_one,
                g_shift_one,
                g_down_b,
                g_gain_two,
                g_shift_two,
                g_up_b,
            )
        ]
    )
    pairs = ((tokens, d_qkv), (context, d_attn_b), (hidden_b, d_pre_b), (activation, d_ffn_b))
    if in_kernels:
        parts = [grad_rows(left, right).astype(jnp.bfloat16) for left, right in pairs]
        parts = [p.reshape((GROUP, -1, p.shape[1])) for p in parts]
        owned = scatter_all(parts + [sums.astype(jnp.bfloat16)])
    else:
        owned = [
            lax.psum_scatter(p, AXIS, scatter_dimension=0, tiled=True)
            for p in [grad_rows(left, right) for left, right in pairs]
            + [sums.reshape((-1, sums.shape[2]))]
        ]
    grad_qkv, grad_outmat, grad_upmat, grad_downmat, vec = owned
    owned_sums = [vec[j, : v.shape[0]] for j, v in enumerate(owned_vectors)]
    return (
        layer_out,
        token_grad,
        grad_qkv,
        owned_sums[0],
        owned_sums[1],
        grad_outmat,
        owned_sums[2],
        owned_sums[3],
        owned_sums[4],
        grad_upmat,
        owned_sums[8],
        grad_downmat,
        owned_sums[5],
        owned_sums[6],
        owned_sums[7],
    )


def solution(mesh):
    placed = (
        P("fsdp", None),
        P("fsdp"),
        P("fsdp"),
        P("fsdp", None),
        P("fsdp"),
        P("fsdp"),
        P("fsdp", None),
        P("fsdp"),
        P("fsdp"),
        P("fsdp"),
        P("fsdp", None),
        P("fsdp"),
        P("fsdp", None),
        P("fsdp"),
        P("fsdp"),
        P("fsdp"),
        P("fsdp", None),
    )
    return jax.shard_map(
        local,
        mesh=mesh,
        in_specs=placed,
        out_specs=(
            P("fsdp", None),
            P("fsdp", None),
            P("fsdp", None),
            P("fsdp"),
            P("fsdp"),
            P("fsdp", None),
            P("fsdp"),
            P("fsdp"),
            P("fsdp"),
            P("fsdp", None),
            P("fsdp"),
            P("fsdp", None),
            P("fsdp"),
            P("fsdp"),
            P("fsdp"),
        ),
        check_vma=False,
    )
```

profile of v0, /device:TPU:1, one launch (start us, length us, event | category | flops | bytes accessed | tf_op | source)
XLA Modules:
  0.0 204.4 jit_solution(12661040819680767405)
XLA Ops:
  4.0 1.2 stack.93
  5.2 68.6 %gather_all.1 = (bf16[32,24,2304]{2,1,0:T(8,128)(2,1)}, bf16[32,24,768]{2,1,0:T(8,128)(2,1)}, bf16[32,24,3072]{2,1,0:T(8,128)(2,1)}, bf16[32,96,768]{2,1,0:T(8,128)(2,1)}, bf16[32,16,128]{2,1,0:T(8,128)(2,1)}) custom-call(bf16[24,2304]{1,0:T(8,128)(2,1)} %refs_0_.1, bf16[24,768]{1,0:T(8,128)(2,1)} %refs_1_.1, bf16[24,3072]{1,0:T(8,128)(2,1)} %refs_2_.1, ...), custom_call_target="tpu_custom_call" | custom-call | tf_op jit(solution)/shard_map/gather_all/pallas_call | solution.py:113
  73.9 1.9 convert_reduce_fusion.1
  75.9 0.9 convert_reduce_fusion.3
  77.2 2.8 %fusion.1.qkv_ref = bf16[128,2304]{1,0:T(8,128)(2,1)S(1)} fusion(bf16[128,768]{1,0:T(8,128)(2,1)} %param.17, bf16[768,2304]{1,0:T(8,128)(2,1)} %bitcast.114, f32[2304]{0:T(1024)S(1)} %pad_maximum_fusion), kind=kOutput, calls=%fused_computation.7 | convolution fusion | flops 453574656 | bytes 4334592 | tf_op jit(solution)/shard_map/dot_general | solution.py:388
  82.8 3.2 %convolution_add_fusion.1 = f32[128,3072]{1,0:T(8,128)S(1)} fusion(bf16[768,3072]{1,0:T(8,128)(2,1)} %bitcast.110, f32[3072]{0:T(1024)S(1)} %reshape.277, f32[128,768]{1,0:T(8,128)S(1)} %get-tuple-element.75, f32[768]{0:T(1024)S(1)} %reshape.276, f32[768]{0:T(1024)S(1)} %reshape.275, f32[128]{0:T(128)S(1)} %add_rsqrt_fusion.1, ...), kind=kOutput, calls=%fused_computation.5 | convolution fusion | flops 604864512 | bytes 6704128 | tf_op jit(solution)/shard_map/dot_general | solution.py:414
  86.1 3.4 %fusion.34 = (f32[128]{0:T(128)S(1)}, f32[128,768]{1,0:T(8,128)S(1)}) fusion(f32[768]{0:T(1024)S(1)} %reshape.278, bf16[3072,768]{1,0:T(8,128)(2,1)} %bitcast.117, f32[128,3072]{1,0:T(8,128)S(1)} %convolution_add_fusion.1, f32[768]{0:T(1024)S(1)} %reshape.276, f32[768]{0:T(1024)S(1)} %reshape.275, f32[128]{0:T(128)S(1)} %add_rsqrt_fusion.1, ...), kind=kOutput, calls=%fused_computation.112 | convolution fusion | flops 606633856 | bytes 7088640 | tf_op jit(solution)/shard_map/dot_general | solution.py:419
  91.1 4.7 %fusion.35 = (bf16[3072]{0:T(1024)(128)(2,1)S(1)}, bf16[128,3072]{1,0:T(8,128)(2,1)S(1)}) fusion(f32[128,3072]{1,0:T(8,128)S(1)} %convolution_add_fusion.1, bf16[3072,768]{1,0:T(8,128)(2,1)} %bitcast.118, f32[128,768]{1,0:T(8,128)S(1)} %get-tuple-element.57), kind=kOutput, calls=%fused_computation.113 | convolution fusion | flops 608400384 | bytes 7477248 | tf_op jit(solution)/shard_map/rd,fd->rf/dot_general | solution.py:431
  95.8 1.8 multiply_reduce_fusion
  97.8 1.1 copy-done.3
  99.5 5.8 %attention_back.1 = (bf16[128,2304]{1,0:T(8,128)(2,1)S(1)}, f32[2,768]{1,0:T(2,128)S(1)}) custom-call(bf16[128,2304]{1,0:T(8,128)(2,1)S(1)} %fusion.1.qkv_ref, bf16[128,768]{1,0:T(8,128)(2,1)S(1)} %convolution_convert_fusion.4.back_ref, s32[128,1]{1,0:T(8,128)S(1)} %copy.43.doc_col, s32[1,128]{1,0:T(1,128)S(1)} %bitcast.105, s32[1,128]{1,0:T(1,128)S(1)} %bitcast.106), custom_call_target="tpu_custom_call" | custom-call | tf_op jit(solution)/shard_map/attention_back/pallas_call | solution.py:311
  105.4 4.0 %convolution_add_fusion.3 = f32[128,768]{1,0:T(8,128)} fusion(f32[128,768]{1,0:T(8,128)S(1)} %get-tuple-element.59, bf16[128,2304]{1,0:T(8,128)(2,1)S(1)} %get-tuple-element.32, bf16[768,2304]{1,0:T(8,128)(2,1)} %bitcast.115), kind=kOutput, calls=%fused_computation.20 | convolution fusion | flops 453083136 | bytes 4915200 | tf_op jit(solution)/shard_map/re,de->rd/dot_general | solution.py:446
  109.4 2.9 %convolution_convert_fusion.2 = bf16[2304,768]{0,1:T(8,128)(2,1)} fusion(bf16[128,2304]{1,0:T(8,128)(2,1)S(1)} %get-tuple-element.32, bf16[128,768]{1,0:T(8,128)(2,1)S(1)} %copy-done.8), kind=kOutput, calls=%fused_computation.2 | convolution fusion | flops 454754304 | bytes 4325376 | tf_op jit(solution)/shard_map/ra,rb->ab/dot_general | solution.py:323
  112.3 1.5 convolution_convert_fusion.3
  113.8 3.6 %convolution_convert_fusion.1 = bf16[768,3072]{1,0:T(8,128)(2,1)} fusion(bf16[128,3072]{1,0:T(8,128)(2,1)S(1)} %copy-done.7, f32[128,768]{1,0:T(8,128)S(1)} %get-tuple-element.75, f32[768]{0:T(1024)S(1)} %reshape.276, f32[768]{0:T(1024)S(1)} %reshape.275, f32[128]{0:T(128)S(1)} %add_rsqrt_fusion.1, f32[128]{0:T(128)S(1)} %broadcast_multiply_fusion.5), kind=kOutput, calls=%fused_computation.1 | convolution fusion | flops 606830592 | bytes 5905408 | tf_op jit(solution)/shard_map/ra,rb->ab/dot_general | solution.py:323
  117.4 3.6 %convolution_convert_fusion = bf16[3072,768]{1,0:T(8,128)(2,1)} fusion(f32[128,768]{1,0:T(8,128)S(1)} %copy-done.5, f32[128,3072]{1,0:T(8,128)S(1)} %convolution_add_fusion.1), kind=kOutput, calls=%fused_computation | convolution fusion | flops 608403456 | bytes 6684672 | tf_op jit(solution)/shard_map/ra,rb->ab/dot_general | solution.py:323
  122.4 1.5 stack.105.refs_4_
  123.9 71.2 %scatter_all.1 = (f32[24,2304]{1,0:T(8,128)}, f32[24,768]{1,0:T(8,128)}, f32[24,3072]{1,0:T(8,128)}, f32[96,768]{1,0:T(8,128)}, f32[16,128]{1,0:T(8,128)}) custom-call(bf16[32,24,2304]{2,1,0:T(8,128)(2,1)} %bitcast.109, bf16[32,24,768]{2,1,0:T(8,128)(2,1)} %bitcast.116, bf16[32,24,3072]{2,1,0:T(8,128)(2,1)} %bitcast.108, bf16[32,96,768]{2,1,0:T(8,128)(2,1)} %bitcast.107, ...), custom_call_target="tpu_custom_call" | custom-call | tf_op jit(solution)/shard_map/scatter_all/pallas_call | solution.py:209
  195.1 1.5 slice_bitcast_fusion
  196.7 1.2 slice_bitcast_fusion.3
  197.9 1.6 copy.59
  199.5 1.5 copy.60
  201.0 1.7 copy.61
  202.7 1.7 copy.62
  (108 shorter events, 10.1 us)
Async XLA Ops:
  79.9 0.7 copy-start.1
  79.9 0.7 copy-start
  80.7 1.3 copy-start.2
  80.7 1.3 copy-start.8
  81.5 1.3 copy-start.9
  86.0 3.7 %copy-start.11 = (bf16[128,768]{1,0:T(8,128)(2,1)S(1)}, bf16[128,768]{1,0:T(8,128)(2,1)}, u32[]{:S(2)}) copy-start(bf16[128,768]{1,0:T(8,128)(2,1)} %param.33) | copy-start | bytes 589828
  90.2 5.6 %slice-start = ((s8[4718592]{0:T(1024)(128)(4,1)}), s8[4194304]{0:T(1024)(128)(4,1)S(1)}, s32[]{:S(2)}) async-start(s8[4718592]{0:T(1024)(128)(4,1)} %bitcast.111), calls=%async_computation | async-start | bytes 8388608
  91.1 4.7 %copy-start.4 = (f32[128,768]{1,0:T(8,128)}, f32[128,768]{1,0:T(8,128)S(1)}, u32[]{:S(2)}) copy-start(f32[128,768]{1,0:T(8,128)S(1)} %get-tuple-element.57) | copy-start | bytes 1179652
  91.1 4.7 %slice-start.1 = ((s8[4718592]{0:T(1024)(128)(4,1)}), s8[524288]{0:T(1024)(128)(4,1)S(1)}, s32[]{:S(2)}) async-start(s8[4718592]{0:T(1024)(128)(4,1)} %bitcast.111), calls=%async_computation.1 | async-start | bytes 1048576
  95.7 1.9 copy-start.6
  97.6 1.3 copy-start.3
  109.4 2.9 %copy-start.10 = (bf16[12,64,128]{2,1,0:T(8,128)(2,1)S(1)}, bf16[12,64,128]{2,1,0:T(8,128)(2,1)}, u32[]{:S(2)}) copy-start(bf16[12,64,128]{2,1,0:T(8,128)(2,1)} %copy-done.9) | copy-start | bytes 589828
  112.3 1.5 copy-start.7
  113.8 3.6 %copy-start.5 = (f32[128,768]{1,0:T(8,128)S(1)}, f32[128,768]{1,0:T(8,128)}, u32[]{:S(2)}) copy-start(f32[128,768]{1,0:T(8,128)} %copy-done.4) | copy-start | bytes 1179652
  117.4 4.6 %copy-start.12 = (bf16[128,768]{1,0:T(8,128)(2,1)S(1)}, bf16[128,768]{1,0:T(8,128)(2,1)}, u32[]{:S(2)}) copy-start(bf16[128,768]{1,0:T(8,128)(2,1)} %param.33) | copy-start | bytes 589828
where the time goes:
time: 206 us; the launch traced here: 204 us
  Pallas kernels  146 us (71%)
  matrix products  33.1 us (16%)
  local copies, waits for them, and re-layouts  19.5 us (9%)
  other arithmetic  4.85 us (2%)
    pallas_call x1, Pallas kernels, scatter_all(): pl.pallas_call(functools.partial(scatter_kernel, count), out_shape=[jax.S...  71.2 us
    pallas_call x1, Pallas kernels, gather_all(): pl.pallas_call(functools.partial(gather_kernel, count), out_shape=[jax.Sh...  68.6 us
    dot_general x4, matrix products, grad_rows(): jnp.einsum('ra,rb->ab', left, right, preferred_element_type=jnp.float32)  11.7 us
    unnamed x34, local copies, waits for them, and re-layouts  8.25 us
    another operation x31, local copies, waits for them, and re-layouts, vector_rows(): return jnp.stack(rows, axis=1)  6.36 us
    pallas_call x1, Pallas kernels, attention_back(): pl.pallas_call(functools.partial(attention_back_kernel, 1.0 / math.sqrt(w...  5.81 us
    dot_general x1, matrix products, local(): jnp.einsum('rd,fd->rf', d_ffn_b, downm_back, preferred_element_type=fl)  4.67 us

commit v1 on v0

--- a/solution.py
+++ b/solution.py
@@ -1,5 +1,7 @@
 import functools
+import heapq
 import math
+import types
 
 import jax
 import jax.numpy as jnp
@@ -11,216 +13,7 @@
 HEADS = 12
 AXIS = "fsdp"
 MESH_IDS = pl.DeviceIdType.MESH
-BITS = 5
 GROUP = 32
-CORE, X, Y, Z1, Z2 = 0, 1, 2, 3, 4
-SCATTER_ORDERS = (
-    (CORE, X, Y, Z1, Z2),
-    (CORE, X, Y, Z1, Z2),
-    (CORE, Y, X, Z1, Z2),
-    (CORE, Z1, Z2, X, Y),
-    (CORE, Z1, Z2, X, Y),
-)
-VMEM_BYTES = 60 * 1024 * 1024
-
-
-def bits_of(me):
-    return [lax.rem(lax.div(me, 1 << b), 2) for b in range(BITS)]
-
-
-def toggled(me, mine, r):
-    for b in range(BITS):
-        if r >> b & 1:
-            me = me + (1 << b) * (1 - 2 * mine[b])
-    return me
-
-
-def greet(me, mine):
-    barrier = pltpu.get_barrier_semaphore()
-    for b in range(BITS):
-        pl.semaphore_signal(
-            barrier, inc=1, device_id=(toggled(me, mine, 1 << b),), device_id_type=MESH_IDS
-        )
-    pl.semaphore_wait(barrier, BITS)
-
-
-def gather_kernel(count, *refs):
-    shards, wholes = refs[:count], refs[count : 2 * count]
-    send_sem, recv_sem, local_sem = refs[2 * count :]
-    me = lax.axis_index(AXIS)
-    mine = bits_of(me)
-    greet(me, mine)
-
-    def move(k, r, b):
-        owner = toggled(me, mine, r)
-        source = shards[k] if r == 0 else wholes[k].at[owner]
-        slot = r | (1 << b)
-        return pltpu.make_async_remote_copy(
-            src_ref=source,
-            dst_ref=wholes[k].at[owner],
-            send_sem=send_sem.at[k, slot],
-            recv_sem=recv_sem.at[k, slot],
-            device_id=(toggled(me, mine, 1 << b),),
-            device_id_type=MESH_IDS,
-        )
-
-    def landed(k, r):
-        here = wholes[k].at[toggled(me, mine, r)]
-        pltpu.make_async_remote_copy(
-            src_ref=here,
-            dst_ref=here,
-            send_sem=send_sem.at[k, r],
-            recv_sem=recv_sem.at[k, r],
-            device_id=(toggled(me, mine, 1),),
-            device_id_type=MESH_IDS,
-        ).wait_recv()
-
-    orders = [tuple(reversed(SCATTER_ORDERS[k])) for k in range(count)]
-    own = [
-        pltpu.make_async_copy(shards[k], wholes[k].at[me], local_sem.at[k]) for k in range(count)
-    ]
-    sent = [[] for _ in range(count)]
-    for k in range(count):
-        for b in orders[k]:
-            copy = move(k, 0, b)
-            copy.start()
-            sent[k].append(copy)
-    for copy in own:
-        copy.start()
-    have = [[0] for _ in range(count)]
-    for step in range(BITS):
-        width = 1 << step
-        for i in range(width):
-            for k in range(count):
-                b = orders[k][step]
-                r = have[k][i] | (1 << b)
-                landed(k, r)
-                for later in orders[k][step + 1 :]:
-                    copy = move(k, r, later)
-                    copy.start()
-                    sent[k].append(copy)
-        for k in range(count):
-            b = orders[k][step]
-            have[k] = have[k] + [r | (1 << b) for r in have[k]]
-    for k in range(count):
-        own[k].wait()
-        for copy in sent[k]:
-            copy.wait_send()
-
-
-def gather_all(shards):
-    count = len(shards)
-    return pl.pallas_call(
-        functools.partial(gather_kernel, count),
-        out_shape=[jax.ShapeDtypeStruct((GROUP,) + s.shape, s.dtype) for s in shards],
-        in_specs=[pl.BlockSpec(memory_space=pl.ANY)] * count,
-        out_specs=[pl.BlockSpec(memory_space=pl.ANY)] * count,
-        scratch_shapes=[
-            pltpu.SemaphoreType.DMA((count, GROUP)),
-            pltpu.SemaphoreType.DMA((count, GROUP)),
-            pltpu.SemaphoreType.DMA((count,)),
-        ],
-        compiler_params=pltpu.CompilerParams(collective_id=0, has_side_effects=True),
-        name="gather_all",
-    )(*shards)
-
-
-def priority(order, step):
-    left = order[step + 1 :]
-    blocks = [0]
-    for b in reversed(left):
-        blocks = [r | (1 << b) for r in blocks] + blocks
-    return blocks
-
-
-def scatter_kernel(count, *refs):
-    parts, outs = refs[:count], refs[count : 2 * count]
-    landing = refs[2 * count : 3 * count]
-    send_sem, recv_sem = refs[3 * count :]
-    me = lax.axis_index(AXIS)
-    mine = bits_of(me)
-    greet(me, mine)
-
-    slot_of = []
-    for k in range(count):
-        table, used = {}, 0
-        for step in range(BITS):
-            for r in priority(SCATTER_ORDERS[k], step):
-                table[step, r] = used
-                used += 1
-        slot_of.append(table)
-
-    def held(k, step, r):
-        if step < 0:
-            return parts[k].at[toggled(me, mine, r)]
-        return landing[k].at[slot_of[k][step, r]]
-
-    def move(k, step, r):
-        b = SCATTER_ORDERS[k][step]
-        slot = slot_of[k][step, r & ~(1 << b)]
-        return pltpu.make_async_remote_copy(
-            src_ref=held(k, step - 1, r),
-            dst_ref=landing[k].at[slot],
-            send_sem=send_sem.at[k, slot],
-            recv_sem=recv_sem.at[k, slot],
-            device_id=(toggled(me, mine, 1 << b),),
-            device_id_type=MESH_IDS,
-        )
-
-    copies = {}
-    for i in range(GROUP // 2):
-        for k in range(count):
-            order = SCATTER_ORDERS[k]
-            r = priority(order, 0)[i]
-            copy = move(k, 0, r | (1 << order[0]))
-            copy.start()
-            copies[k, 0, r] = copy
-    for step in range(BITS):
-        for i in range(1 << (BITS - 1 - step)):
-            for k in range(count):
-                order = SCATTER_ORDERS[k]
-                r = priority(order, step)[i]
-                copies[k, step, r].wait_recv()
-                before, now = held(k, step - 1, r), held(k, step, r)
-                columns = now.shape[-1]
-                last = step == BITS - 1
-                tile = min(columns, 768 if now.shape[0] <= 24 else 256)
-
-                def add(j, carry, before=before, now=now, tile=tile, last=last, k=k):
-                    at = pl.ds(pl.multiple_of(j * tile, tile), tile)
-                    total = now[:, at].astype(jnp.float32) + before[:, at].astype(jnp.float32)
-                    if last:
-                        outs[k][:, at] = total
-                    else:
-                        now[:, at] = total.astype(jnp.bfloat16)
-                    return carry
-
-                lax.fori_loop(0, columns // tile, add, 0)
-                if not last and r >> order[step + 1] & 1:
-                    copy = move(k, step + 1, r)
-                    copy.start()
-                    copies[k, step + 1, r & ~(1 << order[step + 1])] = copy
-    for copy in copies.values():
-        copy.wait_send()
-
-
-def scatter_all(parts):
-    count = len(parts)
-    return pl.pallas_call(
-        functools.partial(scatter_kernel, count),
-        out_shape=[jax.ShapeDtypeStruct(p.shape[1:], jnp.float32) for p in parts],
-        in_specs=[pl.BlockSpec(memory_space=pltpu.VMEM)] * count,
-        out_specs=[pl.BlockSpec(memory_space=pltpu.VMEM)] * count,
-        scratch_shapes=[pltpu.VMEM((GROUP - 1,) + p.shape[1:], p.dtype) for p in parts]
-        + [
-            pltpu.SemaphoreType.DMA((count, GROUP)),
-            pltpu.SemaphoreType.DMA((count, GROUP)),
-        ],
-        compiler_params=pltpu.CompilerParams(
-            collective_id=1, has_side_effects=True, vmem_limit_bytes=VMEM_BYTES
-        ),
-        name="scatter_all",
-    )(*parts)
 
 
 norm_eps = 1e-06
@@ -323,6 +116,757 @@
     return jnp.einsum("ra,rb->ab", left, right, preferred_element_type=jnp.float32)
 
 
+X, Y, Z1, Z2 = 0, 1, 2, 3
+GATHER_ORDERS = (
+    (Z2, Z1, X, Y),
+    (Z2, Z1, Y, X),
+    (X, Z2, Z1, Y),
+    (Y, Z2, Z1, X),
+    (Z2, Z1, X, Y),
+)
+SCATTER_ORDERS = tuple(tuple(reversed(o)) for o in GATHER_ORDERS)
+PAIRS = 16
+PIECE_ROWS = (48, 48, 48, 192, 32)
+PIECE_COLS = (1152, 384, 1536, 384, 128)
+COUNT = 5
+HOPS = {X: ((0, 1),), Y: ((1, 1),), Z1: ((2, 1),), Z2: ((2, 1), (3, 2))}
+LINK_BYTES_PER_US = 46e3
+HOP_US = 1.0
+FUSED_VMEM = 58 * 1024 * 1024
+
+
+class Plan:
+    def __init__(self):
+        self.now = 0.0
+        self.free = {}
+        self.pending = []
+        self.seq = 0
+
+    def travel(self, dim, size, key):
+        us = size / LINK_BYTES_PER_US
+        begin = max([self.now] + [self.free.get(link, 0.0) for link, _ in HOPS[dim]])
+        end = begin
+        for link, cost in HOPS[dim]:
+            self.free[link] = begin + cost * us
+            end = max(end, begin + cost * us)
+        heapq.heappush(self.pending, (end + HOP_US, self.seq, key))
+        self.seq += 1
+
+
+def subsets(order, step):
+    blocks = [0]
+    for b in reversed(order[step + 1 :]):
+        blocks = [r | (1 << b) for r in blocks] + blocks
+    return blocks
+
+
+def dot(a, b, over=((1,), (0,))):
+    return lax.dot_general(a, b, (over, ((), ())), preferred_element_type=jnp.float32)
+
+
+ROWS_BOTH, COLS_BOTH = ((0,), (0,)), ((1,), (1,))
+
+SIBLING_COPIES = 25
+
+
+def scratch_of(rows, width, hidden):
+    fl, bf = jnp.float32, jnp.bfloat16
+    both, half, hhalf = 2 * rows, width // 2, hidden // 2
+    lists = []
+    for shape_of in (
+        lambda pr, pc: ((PAIRS * pr, pc), bf),
+        lambda pr, pc: ((PAIRS * pr, pc), bf),
+        lambda pr, pc: ((PAIRS - 1, pr, pc), bf),
+        lambda pr, pc: (((pr // 2 + 15) // 16 * 16, pc), bf),
+        lambda pr, pc: (((pr // 2 + 15) // 16 * 16, pc), bf),
+        lambda pr, pc: ((pr, pc), fl),
+    ):
+        lists += [shape_of(PIECE_ROWS[k], PIECE_COLS[k]) for k in range(COUNT)]
+    named = dict(
+        peer_part4=((PAIRS * PIECE_ROWS[4], PIECE_COLS[4]), bf),
+        stage_part4=((PAIRS * PIECE_ROWS[4], PIECE_COLS[4]), bf),
+        tok=((both, width), bf),
+        marks=((2, 8, rows), fl),
+        vec32=((PAIRS * 32, 128), fl),
+        vecs=((16, width), fl),
+        upb=((8, hhalf), fl),
+        qkv=((both, 3 * half), bf),
+        probs=((HEADS, rows, rows), fl),
+        ctx=((both, width), bf),
+        proj_s=((rows, half), fl),
+        proj_r=((rows, half), fl),
+        proj_o=((rows, half), fl),
+        hid=((rows, width), fl),
+        n1=((rows, width), fl),
+        i1=((rows, 128), fl),
+        hb=((both, width), bf),
+        act=((both, hidden), bf),
+        fac=((both, hhalf), fl),
+        ffn_s=((rows, half), fl),
+        ffn_r=((rows, half), fl),
+        ffn_o=((rows, half), fl),
+        dff=((rows, width), fl),
+        dfb=((both, width), bf),
+        dact_s=((both, hhalf), fl),
+        dact_r=((both, hhalf), fl),
+        dact_o=((both, hhalf), fl),
+        dpre=((both, hhalf), bf),
+        dhid_s=((rows, width), fl),
+        dhid_r=((rows, width), fl),
+        dhid_o=((rows, width), fl),
+        dat=((rows, width), fl),
+        datb=((both, width), bf),
+        dctx_s=((both, half), fl),
+        dctx_r=((both, half), fl),
+        dctx_o=((both, half), fl),
+        dctx=((both, half), bf),
+        dqkv=((both, 3 * half), bf),
+        tg_s=((rows, width), fl),
+        tg_r=((rows, width), fl),
+        tg_o=((rows, width), fl),
+        sums=((16, width), fl),
+        upsum=((8, hhalf), fl),
+    )
+    return lists, named
+
+
+def layer_kernel(names, *refs):
+    refs = list(refs)
+
+    def take(count):
+        taken, refs[:count] = refs[:count], []
+        return taken
+
+    R = types.SimpleNamespace()
+    R.tokens, R.doc, R.pad = take(3)
+    R.w, R.v, R.cotangent = take(4), take(9), take(1)[0]
+    R.layer_out, R.token_grad = take(2)
+    R.g, R.gv = take(4), take(1)[0]
+    R.whole, R.part, R.land, R.stage, R.peer, R.fin = (take(COUNT) for _ in range(6))
+    vars(R).update(zip(names, take(len(names))))
+    sib_send, sib_recv, g_send, g_recv, s_send, s_recv = refs
+    fl, bf = jnp.float32, jnp.bfloat16
+    rows, width = R.tokens.shape
+    hidden = R.w[2].shape[1]
+    half, hhalf = width // 2, hidden // 2
+    size = width // HEADS
+    scale = 1.0 / math.sqrt(size)
+    me = lax.axis_index(AXIS)
+    core = lax.rem(me, 2)
+    pair = lax.div(me, 2)
+    bits = [lax.rem(lax.div(pair, 1 << b), 2) for b in range(4)]
+    sibling = me + 1 - 2 * core
+    is_first = core == 0
+
+    def pair_of(r):
+        p = pair
+        for b in range(4):
+            if r >> b & 1:
+                p = p + (1 << b) * (1 - 2 * bits[b])
+        return p
+
+    def device_along(b):
+        return me + (2 << b) * (1 - 2 * bits[b])
+
+    def by_core(step, which=None):
+        at = core if which is None else 1 - core
+        return pl.multiple_of(at * step, step)
+
+    own_rows, sib_rows = pl.ds(by_core(rows), rows), pl.ds(by_core(rows, 1), rows)
+    own_half, sib_half = pl.ds(by_core(half), half), pl.ds(by_core(half, 1), half)
+    own_hh, sib_hh = pl.ds(by_core(hhalf), hhalf), pl.ds(by_core(hhalf, 1), hhalf)
+
+    barrier = pltpu.get_barrier_semaphore()
+    for other in [sibling] + [device_along(b) for b in range(4)]:
+        pl.semaphore_signal(barrier, inc=1, device_id=(other,), device_id_type=MESH_IDS)
+    pl.semaphore_wait(barrier, 5)
+
+    sib = {}
+    sent = []
+
+    def to_sibling(i, src, dst):
+        copy = pltpu.make_async_remote_copy(
+            src_ref=src,
+            dst_ref=dst,
+            send_sem=sib_send.at[i],
+            recv_sem=sib_recv.at[i],
+            device_id=(sibling,),
+            device_id_type=MESH_IDS,
+        )
+        copy.start()
+        sib[i] = copy
+        sent.append(copy)
+
+    def side_by_side(own, other):
+        return jnp.concatenate(
+            [jnp.where(is_first, own, other), jnp.where(is_first, other, own)], axis=1
+        )
+
+    def shard_half(k, mine):
+        ref = R.w[k]
+        if k == 0:
+            cols = [
+                ref[:, pl.ds(pl.multiple_of(p * width + (core if mine else 1 - core) * half, 128), half)]
+                for p in range(3)
+            ]
+            return jnp.concatenate([c.astype(fl) for c in cols], axis=1)
+        cols = PIECE_COLS[k]
+        return ref[:, pl.ds(by_core(cols, None if mine else 1), cols)].astype(fl)
+
+    def padded(value):
+        short = -value.shape[0] % 16
+        if short:
+            value = jnp.concatenate([value, jnp.zeros((short, value.shape[1]), fl)], axis=0)
+        return value.astype(bf)
+
+    R.stage[4][...] = jnp.zeros(R.stage[4].shape, bf)
+    R.vec32[pl.ds(0, 16), :] = jnp.zeros((16, 128), fl)
+    for j in range(9):
+        v = R.v[j]
+        R.vec32[j : j + 1, 0 : v.shape[1]] = v[...].astype(fl)
+    R.stage[4][...] = R.vec32[pl.ds(0, 16), :].astype(bf)
+    for k in (0, 4, 1, 2, 3):
+        if k < 4:
+            R.stage[k][...] = padded(shard_half(k, False))
+        to_sibling(k, R.stage[k], R.peer[k])
+    to_sibling(5, R.tokens, R.tok.at[own_rows])
+    own_marks = jnp.concatenate(
+        [R.doc[...].astype(fl), R.pad[...].astype(fl), jnp.zeros((6, rows), fl)], axis=0
+    )
+    R.marks[core] = own_marks
+    to_sibling(6, R.marks.at[core], R.marks.at[core])
+    R.tok[own_rows, :] = R.tokens[...]
+
+    plan = Plan()
+    piece_bytes = [2 * PIECE_ROWS[k] * PIECE_COLS[k] for k in range(COUNT)]
+    done = [1] * COUNT
+
+    def piece_at(k, r):
+        n = PIECE_ROWS[k]
+        return pl.ds(pl.multiple_of(pair_of(r) * n, n), n)
+
+    def gather_move(k, r, b):
+        at = piece_at(k, r)
+        slot = r | (1 << b)
+        copy = pltpu.make_async_remote_copy(
+            src_ref=R.whole[k].at[at],
+            dst_ref=R.whole[k].at[at],
+            send_sem=g_send.at[k, slot],
+            recv_sem=g_recv.at[k, slot],
+            device_id=(device_along(b),),
+            device_id_type=MESH_IDS,
+        )
+        copy.start()
+        sent.append(copy)
+        plan.travel(b, piece_bytes[k], (True, k, slot, b))
+
+    for k in (0, 4, 1, 2, 3):
+        sib[k].wait_recv()
+        if k < 4:
+            mine = shard_half(k, True)
+        else:
+            mine = R.vec32[pl.ds(0, 16), :]
+        theirs = R.peer[k][...].astype(fl)[: mine.shape[0]]
+        R.whole[k][piece_at(k, 0), :] = jnp.concatenate(
+            [jnp.where(is_first, mine, theirs), jnp.where(is_first, theirs, mine)], axis=0
+        ).astype(bf)
+        for b in GATHER_ORDERS[k]:
+            gather_move(k, 0, b)
+
+    def on_gather(k, r, b):
+        here = R.whole[k].at[piece_at(k, r)]
+        pltpu.make_async_remote_copy(
+            src_ref=here,
+            dst_ref=here,
+            send_sem=g_send.at[k, r],
+            recv_sem=g_recv.at[k, r],
+            device_id=(device_along(b),),
+            device_id_type=MESH_IDS,
+        ).wait_recv()
+        order = GATHER_ORDERS[k]
+        for later in order[order.index(b) + 1 :]:
+            gather_move(k, r, later)
+        done[k] += 1
+
+    slot_of = []
+    for k in range(COUNT):
+        table = {}
+        for step in range(4):
+            for r in subsets(SCATTER_ORDERS[k], step):
+                table[step, r] = len(table)
+        slot_of.append(table)
+    copies = {}
+
+    def held(k, step, r):
+        if step < 0:
+            return R.part[k].at[piece_at(k, r)]
+        return R.land[k].at[slot_of[k][step, r]]
+
+    def scatter_move(k, step, r):
+        b = SCATTER_ORDERS[k][step]
+        low = r & ~(1 << b)
+        slot = slot_of[k][step, low]
+        copy = pltpu.make_async_remote_copy(
+            src_ref=held(k, step - 1, r),
+            dst_ref=R.land[k].at[slot],
+            send_sem=s_send.at[k, slot],
+            recv_sem=s_recv.at[k, slot],
+            device_id=(device_along(b),),
+            device_id_type=MESH_IDS,
+        )
+        copy.start()
+        sent.append(copy)
+        copies[k, step, low] = copy
+        plan.travel(b, piece_bytes[k], (False, k, step, low))
+
+    def scatter_start(k):
+        order = SCATTER_ORDERS[k]
+        for r in subsets(order, 0):
+            scatter_move(k, 0, r | (1 << order[0]))
+
+    def finish(k):
+        if k == 4:
+            R.gv[...] = R.fin[4][pl.ds(by_core(16), 16), :]
+            return
+        n = PIECE_ROWS[k] // 2
+        mine = R.fin[k].at[pl.ds(by_core(n), n)]
+        theirs = R.fin[k].at[pl.ds(by_core(n, 1), n)]
+        if k == 0:
+            for p in range(3):
+                at = pl.ds(pl.multiple_of(p * width + core * half, 128), half)
+                part = pl.ds(p * half, half)
+                to_sibling(18 + p, theirs.at[:, part], R.g[0].at[:, at])
+                R.g[0][:, at] = mine[:, part]
+        else:
+            at = pl.ds(by_core(PIECE_COLS[k]), PIECE_COLS[k])
+            to_sibling(20 + k, theirs, R.g[k].at[:, at])
+            R.g[k][:, at] = mine[...]
+
+    summed = set()
+    early = {}
+
+    def on_scatter(k, step, r):
+        if step and (k, step - 1, r) not in summed:
+            early[k, step - 1, r] = step
+            return
+        summed.add((k, step, r))
+        add_piece(k, step, r)
+        if (k, step, r) in early:
+            on_scatter(k, early[k, step, r], r)
+
+    def add_piece(k, step, r):
+        copies[k, step, r].wait_recv()
+        order = SCATTER_ORDERS[k]
+        before, now = held(k, step - 1, r), held(k, step, r)
+        total = now[...].astype(fl) + before[...].astype(fl)
+        if step == 3:
+            R.fin[k][...] = total
+            finish(k)
+            return
+        now[...] = total.astype(bf)
+        if r >> order[step + 1] & 1:
+            scatter_move(k, step + 1, r)
+
+    def column_of(n, period):
+        return jnp.floor((n + 0.5) * (1.0 / period))
+
+    def pick(count, period):
+        n = lax.broadcasted_iota(jnp.int32, (128, count), 1).astype(fl)
+        i = lax.broadcasted_iota(jnp.int32, (128, count), 0).astype(fl)
+        return jnp.where(n - period * column_of(n, period) == i, 1.0, 0.0).astype(bf)
+
+    def owner_is(count, period, first):
+        n = lax.broadcasted_iota(jnp.int32, (GROUP, count), 1).astype(fl)
+        d = lax.broadcasted_iota(jnp.int32, (GROUP, count), 0).astype(fl)
+        return column_of(n, period) + first == d
+
+    small, large = width // GROUP, hidden // GROUP
+
+    def half_first():
+        return jnp.where(is_first, 0.0, GROUP / 2.0)
+
+    def task_vectors():
+        R.vec32[...] = R.whole[4][...].astype(fl)
+        chosen, owner = pick(width, small), owner_is(width, small, 0.0)
+        for j in range(8):
+            v = R.vec32[pl.ds(j, GROUP, stride=16), :].astype(bf)
+            R.vecs[j : j + 1, :] = jnp.sum(
+                jnp.where(owner, dot(v, chosen), 0.0), axis=0, keepdims=True
+            )
+        v = R.vec32[pl.ds(8, GROUP, stride=16), :].astype(bf)
+        R.upb[0:1, :] = jnp.sum(
+            jnp.where(owner_is(hhalf, large, half_first()), dot(v, pick(hhalf, large)), 0.0),
+            axis=0,
+            keepdims=True,
+        )
+
+    def vec(j):
+        return R.vecs[j : j + 1, :]
+
+    def task_qkv():
+        sib[5].wait_recv()
+        sib[6].wait_recv()
+        for p in range(3):
+            at = pl.ds(p * half, half)
+            value = dot(R.tok[...], R.whole[0][:, at])
+            if p != 1:
+                value = value + R.vecs[p // 2 : p // 2 + 1, own_half]
+            R.qkv[:, at] = value.astype(bf)
+
+    def seen(b):
+        doc, pad = R.marks[b, 0:1, :], R.marks[b, 1:2, :]
+        square = (rows, rows)
+        wide = jnp.broadcast_to(doc, square)
+        same = lax.broadcasted_iota(jnp.int32, square, 0) == lax.broadcasted_iota(
+            jnp.int32, square, 1
+        )
+        return (wide.T == wide) & ((jnp.broadcast_to(pad, square) == 1.0) | same)
+
+    def head_of(b, h):
+        at = b * rows
+        return [
+            R.qkv[at : at + rows, p * half + h * size : p * half + (h + 1) * size]
+            for p in range(3)
+        ]
+
+    def task_attention(b, two):
+        visible = seen(b)
+        found = []
+        for h in (2 * two, 2 * two + 1):
+            query, key_rows, value_rows = head_of(b, h)
+            scores = jnp.where(visible, dot(query, key_rows, COLS_BOTH) * scale, -1e30)
+            row_max = jnp.max(scores, axis=-1, keepdims=True)
+            total = jnp.sum(jnp.exp(scores - row_max), axis=-1, keepdims=True)
+            probs = jnp.exp(scores - (row_max + jnp.log(total)))
+            R.probs[b * (HEADS // 2) + h] = probs
+            found.append(dot(probs.astype(bf), value_rows))
+        at = pl.ds(pl.multiple_of(core * half + two * 2 * size, 128), 2 * size)
+        R.ctx[pl.ds(b * rows, rows), at] = jnp.concatenate(found, axis=1).astype(bf)
+        if b == 1 and two == HEADS // 4 - 1:
+            to_sibling(7, R.ctx.at[:, own_half], R.ctx.at[:, own_half])
+
+    def task_project():
+        sib[7].wait_recv()
+        R.proj_s[...] = dot(R.ctx[sib_rows, :], R.whole[1][...])
+        to_sibling(8, R.proj_s, R.proj_r)
+        R.proj_o[...] = dot(R.ctx[own_rows, :], R.whole[1][...])
+
+    def norm(values):
+        centred = values - jnp.mean(values, axis=-1, keepdims=True)
+        inverse = lax.rsqrt(jnp.mean(centred * centred, axis=-1, keepdims=True) + norm_eps)
+        return centred * inverse, inverse
+
+    def task_norm_one():
+        sib[8].wait_recv()
+        attn = (
+            R.tokens[...].astype(fl)
+            + side_by_side(R.proj_o[...], R.proj_r[...])
+            + vec(2)
+        )
+        normed, inverse = norm(attn)
+        hid = normed * vec(3) + vec(4)
+        R.n1[...] = normed
+        R.i1[...] = jnp.broadcast_to(inverse, (rows, 128))
+        R.hid[...] = hid
+        R.hb[own_rows, :] = hid.astype(bf)
+        to_sibling(9, R.hb.at[own_rows], R.hb.at[own_rows])
+
+    tile = 384
+
+    def task_up():
+        sib[9].wait_recv()
+
+        def body(t, carry):
+            at = pl.ds(pl.multiple_of(t * tile, tile), tile)
+            pre = dot(R.hb[...], R.whole[2][:, at]) + R.upb[0:1, at]
+            cdf = 0.5 * (1.0 + lax.erf(pre * root_half))
+            pdf = jnp.exp(-0.5 * pre * pre) * inv_root_two_pi
+            R.fac[:, at] = cdf + pre * pdf
+            R.act[:, pl.ds(pl.multiple_of(core * hhalf + t * tile, tile), tile)] = (
+                pre * cdf
+            ).astype(bf)
+            return carry
+
+        lax.fori_loop(0, hhalf // tile, body, 0)
+        to_sibling(10, R.act.at[:, own_hh], R.act.at[:, own_hh])
+
+    def task_ffn():
+        sib[10].wait_recv()
+        R.ffn_s[...] = dot(R.act[sib_rows, :], R.whole[3][...])
+        to_sibling(11, R.ffn_s, R.ffn_r)
+        R.ffn_o[...] = dot(R.act[own_rows, :], R.whole[3][...])
+
+    def back_of_norm(upstream, normed, inverse, gain):
+        scaled = upstream * gain
+        return inverse * (
+            scaled
+            - jnp.mean(scaled, axis=-1, keepdims=True)
+            - normed * jnp.mean(scaled * normed, axis=-1, keepdims=True)
+        )
+
+    def add_sum(j, values):
+        R.sums[j : j + 1, :] = jnp.sum(values, axis=0, keepdims=True)
+
+    def task_norm_two():
+        sib[11].wait_recv()
+        total = R.hid[...] + side_by_side(R.ffn_o[...], R.ffn_r[...]) + vec(5)
+        normed, inverse = norm(total)
+        R.layer_out[...] = (normed * vec(6) + vec(7)).astype(bf)
+        upstream = R.cotangent[...].astype(fl)
+        d_ffn = back_of_norm(upstream, normed, inverse, vec(6))
+        R.dff[...] = d_ffn
+        R.dfb[own_rows, :] = d_ffn.astype(bf)
+        to_sibling(12, R.dfb.at[own_rows], R.dfb.at[own_rows])
+        add_sum(6, upstream * normed)
+        add_sum(7, upstream)
+        add_sum(5, d_ffn)
+
+    def task_grad_down():
+        sib[12].wait_recv()
+
+        def body(t, carry):
+            at = pl.ds(pl.multiple_of(t * tile, tile), tile)
+            R.part[3][at, :] = dot(R.act[:, at], R.dfb[:, own_half], ROWS_BOTH).astype(bf)
+            return carry
+
+        lax.fori_loop(0, hidden // tile, body, 0)
+        scatter_start(3)
+
+    def d_act_half(which, into):
+        def body(t, carry):
+            src = pl.ds(pl.multiple_of(which * hhalf + t * tile, tile), tile)
+            at = pl.ds(pl.multiple_of(t * tile, tile), tile)
+            into[:, at] = dot(R.dfb[:, own_half], R.whole[3][src, :], COLS_BOTH)
+            return carry
+
+        lax.fori_loop(0, hhalf // tile, body, 0)
+
+    def task_d_act():
+        d_act_half(1 - core, R.dact_s)
+        to_sibling(13, R.dact_s, R.dact_r)
+        d_act_half(core, R.dact_o)
+
+    def task_d_pre():
+        sib[13].wait_recv()
+
+        def body(t, carry):
+            at = pl.ds(pl.multiple_of(t * tile, tile), tile)
+            value = (R.dact_o[:, at] + R.dact_r[:, at]) * R.fac[:, at]
+            R.upsum[0:1, at] = jnp.sum(value, axis=0, keepdims=True)
+            R.dpre[:, at] = value.astype(bf)
+            return carry
+
+        lax.fori_loop(0, hhalf // tile, body, 0)
+
+    def task_d_hidden():
+        R.dhid_s[...] = dot(R.dpre[sib_rows, :], R.whole[2][...], COLS_BOTH)
+        to_sibling(14, R.dhid_s, R.dhid_r)
+        R.dhid_o[...] = dot(R.dpre[own_rows, :], R.whole[2][...], COLS_BOTH)
+
+    def task_grad_up():
+        def body(t, carry):
+            at = pl.ds(pl.multiple_of(t * tile, tile), tile)
+            R.part[2][:, at] = dot(R.hb[...], R.dpre[:, at], ROWS_BOTH).astype(bf)
+            return carry
+
+        lax.fori_loop(0, hhalf // tile, body, 0)
+        scatter_start(2)
+
+    def task_norm_one_back():
+        sib[14].wait_recv()
+        d_hid = R.dff[...] + R.dhid_o[...] + R.dhid_r[...]
+        normed = R.n1[...]
+        d_attn = back_of_norm(d_hid, normed, R.i1[:, 0:1], vec(3))
+        R.dat[...] = d_attn
+        R.datb[own_rows, :] = d_attn.astype(bf)
+        to_sibling(15, R.datb.at[own_rows], R.datb.at[own_rows])
+        add_sum(3, d_hid * normed)
+        add_sum(4, d_hid)
+        add_sum(2, d_attn)
+
+    def task_d_context():
+        sib[15].wait_recv()
+        right = R.datb[:, own_half]
+        R.dctx_s[...] = dot(right, R.whole[1][sib_half, :], COLS_BOTH)
+        to_sibling(16, R.dctx_s, R.dctx_r)
+        R.dctx_o[...] = dot(right, R.whole[1][own_half, :], COLS_BOTH)
+
+    def task_grad_out():
+        R.part[1][...] = dot(R.ctx[...], R.datb[:, own_half], ROWS_BOTH).astype(bf)
+        scatter_start(1)
+
+    def task_d_context_sum():
+        sib[16].wait_recv()
+        R.dctx[...] = (R.dctx_o[...] + R.dctx_r[...]).astype(bf)
+
+    bias_sums = {}
+
+    def task_attention_back(b, two):
+        found = []
+        at = b * rows
+        for h in (2 * two, 2 * two + 1):
+            query, key_rows, value_rows = head_of(b, h)
+            back = R.dctx[at : at + rows, h * size : (h + 1) * size]
+            probs = R.probs[b * (HEADS // 2) + h]
+            d_value = dot(probs.astype(bf), back, ROWS_BOTH)
+            d_probs = dot(back, value_rows, COLS_BOTH)
+            delta = jnp.sum(probs * d_probs, axis=-1, keepdims=True)
+            d_scores = (probs * (d_probs - delta) * scale).astype(bf)
+            found.append((dot(d_scores, key_rows), dot(d_scores, query, ROWS_BOTH), d_value))
+        for p in range(3):
+            block = jnp.concatenate([found[0][p], found[1][p]], axis=1)
+            cols = p * half + two * 2 * size
+            R.dqkv[at : at + rows, cols : cols + 2 * size] = block.astype(bf)
+            if p != 1:
+                total = jnp.sum(block, axis=0, keepdims=True)
+                if b == 0:
+                    bias_sums[p, two] = total
+                else:
+                    to = pl.ds(pl.multiple_of(core * half + two * 2 * size, 128), 2 * size)
+                    R.sums[p // 2 : p // 2 + 1, to] = total + bias_sums[p, two]
+
+    def task_clear_sums():
+        R.sums[...] = jnp.zeros(R.sums.shape, fl)
+
+    def task_grad_qkv():
+        for p in range(3):
+            at = pl.ds(p * half, half)
+            R.part[0][:, at] = dot(R.tok[...], R.dqkv[:, at], ROWS_BOTH).astype(bf)
+        scatter_start(0)
+
+    def task_token_grad():
+        R.tg_s[...] = dot(R.dqkv[sib_rows, :], R.whole[0][...], COLS_BOTH)
+        to_sibling(17, R.tg_s, R.tg_r)
+        R.tg_o[...] = R.dat[...] + dot(R.dqkv[own_rows, :], R.whole[0][...], COLS_BOTH)
+
+    def task_sums():
+        chosen, owner = pick(width, small), owner_is(width, small, 0.0)
+        R.vec32[...] = jnp.zeros(R.vec32.shape, fl)
+        for j in range(8):
+            spread = jnp.where(owner, R.sums[j : j + 1, :], 0.0).astype(bf)
+            R.vec32[pl.ds(j, GROUP, stride=16), :] = dot(spread, chosen, COLS_BOTH)
+        spread = jnp.where(
+            owner_is(hhalf, large, half_first()), R.upsum[0:1, :], 0.0
+        ).astype(bf)
+        R.vec32[pl.ds(8, GROUP, stride=16), :] = dot(spread, pick(hhalf, large), COLS_BOTH)
+        R.stage_part4[...] = R.vec32[...].astype(bf)
+        to_sibling(24, R.stage_part4, R.peer_part4)
+
+    def task_sums_send():
+        sib[24].wait_recv()
+        R.part[4][...] = (R.vec32[...] + R.peer_part4[...].astype(fl)).astype(bf)
+        scatter_start(4)
+
+    def task_token_grad_sum():
+        sib[17].wait_recv()
+        R.token_grad[...] = R.tg_o[...] + R.tg_r[...]
+
+    two_heads = [(b, two) for b in range(2) for two in range(HEADS // 4)]
+    tasks = [(task_clear_sums, (), 0.1), (task_vectors, (4,), 0.8), (task_qkv, (0,), 1.2)]
+    tasks += [(functools.partial(task_attention, b, two), (), 1.0) for b, two in two_heads]
+    tasks += [
+        (task_project, (1,), 1.5),
+        (task_norm_one, (), 1.5),
+        (task_up, (2,), 5.0),
+        (task_ffn, (3,), 1.5),
+        (task_norm_two, (), 2.0),
+        (task_grad_down, (), 2.5),
+        (task_d_act, (), 1.5),
+        (task_d_pre, (), 1.5),
+        (task_d_hidden, (), 1.0),
+        (task_grad_up, (), 1.5),
+        (task_norm_one_back, (), 1.0),
+        (task_d_context, (), 1.5),
+        (task_grad_out, (), 0.7),
+        (task_d_context_sum, (), 0.5),
+    ]
+    tasks += [(functools.partial(task_attention_back, b, two), (), 1.0) for b, two in two_heads]
+    tasks += [
+        (task_grad_qkv, (), 1.2),
+        (task_token_grad, (), 1.0),
+        (task_sums, (), 0.8),
+        (task_sums_send, (), 0.8),
+        (task_token_grad_sum, (), 0.3),
+    ]
+    while tasks or plan.pending:
+        soonest = plan.pending[0][0] if plan.pending else None
+        ready = bool(tasks) and all(done[k] == PAIRS for k in tasks[0][1])
+        if plan.pending and (soonest <= plan.now or not ready):
+            plan.now = max(plan.now, soonest)
+            key = heapq.heappop(plan.pending)[2]
+            if key[0]:
+                plan.now += 0.1
+                on_gather(*key[1:])
+            else:
+                plan.now += 0.3
+                on_scatter(*key[1:])
+        else:
+            task, _, cost = tasks.pop(0)
+            plan.now += cost
+            task()
+    for i in range(18, 24):
+        sib[i].wait_recv()
+    for copy in sent:
+        copy.wait_send()
+
+
+def fused(tokens, doc_ids, pad_mask, matrices, vectors, cotangent):
+    rows, width = tokens.shape
+    hidden = matrices[2].shape[1]
+    fl = jnp.float32
+    lists, named = scratch_of(rows, width, hidden)
+    operands = (
+        [tokens, doc_ids[None], pad_mask[None]]
+        + list(matrices)
+        + [v[None] for v in vectors]
+        + [cotangent]
+    )
+    vmem = pl.BlockSpec(memory_space=pltpu.VMEM)
+    dma = pltpu.SemaphoreType.DMA
+    layer_out, token_grad, g0, g1, g2, g3, gv = pl.pallas_call(
+        functools.partial(layer_kernel, tuple(named)),
+        out_shape=[
+            jax.ShapeDtypeStruct(tokens.shape, jnp.bfloat16),
+            jax.ShapeDtypeStruct(tokens.shape, fl),
+        ]
+        + [jax.ShapeDtypeStruct(m.shape, fl) for m in matrices]
+        + [jax.ShapeDtypeStruct((16, 128), fl)],
+        in_specs=[vmem] * len(operands),
+        out_specs=[vmem] * 7,
+        scratch_shapes=[pltpu.VMEM(shape, kind) for shape, kind in lists + list(named.values())]
+        + [
+            dma((SIBLING_COPIES,)),
+            dma((SIBLING_COPIES,)),
+            dma((COUNT, PAIRS)),
+            dma((COUNT, PAIRS)),
+            dma((COUNT, PAIRS)),
+            dma((COUNT, PAIRS)),
+        ],
+        compiler_params=pltpu.CompilerParams(
+            collective_id=0, has_side_effects=True, vmem_limit_bytes=FUSED_VMEM
+        ),
+        name="layer",
+    )(*operands)
+    s = [gv[j, : v.shape[0]] for j, v in enumerate(vectors)]
+    return (
+        layer_out,
+        token_grad,
+        g0,
+        s[0],
+        s[1],
+        g1,
+        s[2],
+        s[3],
+        s[4],
+        g2,
+        s[8],
+        g3,
+        s[5],
+        s[6],
+        s[7],
+    )
+
+
 def local(
     tokens,
     doc_ids,
@@ -343,7 +887,25 @@
     cotangent,
 ):
     fl = jnp.float32
-    in_kernels = lax.axis_size(AXIS) == GROUP
+    if lax.axis_size(AXIS) == GROUP:
+        return fused(
+            tokens,
+            doc_ids,
+            pad_mask,
+            (qkv_matrix, out_matrix, up_matrix, down_matrix),
+            (
+                query_bias,
+                value_bias,
+                out_bias,
+                attn_gain,
+                attn_shift,
+                down_bias,
+                ffn_gain,
+                ffn_shift,
+                up_bias,
+            ),
+            cotangent,
+        )
     owned_vectors = (
         query_bias,
         value_bias,
@@ -356,14 +918,10 @@
         up_bias,
     )
     vectors = vector_rows([v[None] for v in owned_vectors])[0]
-    if in_kernels:
-        wholes = gather_all([qkv_matrix, out_matrix, up_matrix, down_matrix, vectors])
-        wholes = [w.reshape((-1, w.shape[-1])) for w in wholes]
-    else:
-        wholes = [
-            lax.all_gather(w, AXIS, axis=0, tiled=True)
-            for w in (qkv_matrix, out_matrix, up_matrix, down_matrix, vectors)
-        ]
+    wholes = [
+        lax.all_gather(w, AXIS, axis=0, tiled=True)
+        for w in (qkv_matrix, out_matrix, up_matrix, down_matrix, vectors)
+    ]
     qkv_full, outm_full, upm_full, downm_full, vectors_full = wholes
     vectors_full = vectors_full.reshape((-1,) + vectors.shape)
     (
@@ -461,16 +1019,11 @@
         ]
     )
     pairs = ((tokens, d_qkv), (context, d_attn_b), (hidden_b, d_pre_b), (activation, d_ffn_b))
-    if in_kernels:
-        parts = [grad_rows(left, right).astype(jnp.bfloat16) for left, right in pairs]
-        parts = [p.reshape((GROUP, -1, p.shape[1])) for p in parts]
-        owned = scatter_all(parts + [sums.astype(jnp.bfloat16)])
-    else:
-        owned = [
-            lax.psum_scatter(p, AXIS, scatter_dimension=0, tiled=True)
-            for p in [grad_rows(left, right) for left, right in pairs]
-            + [sums.reshape((-1, sums.shape[2]))]
-        ]
+    owned = [
+        lax.psum_scatter(p, AXIS, scatter_dimension=0, tiled=True)
+        for p in [grad_rows(left, right) for left, right in pairs]
+        + [sums.reshape((-1, sums.shape[2]))]
+    ]
     grad_qkv, grad_outmat, grad_upmat, grad_downmat, vec = owned
     owned_sums = [vec[j, : v.shape[0]] for j, v in enumerate(owned_vectors)]
     return (

time: 206 us -> 160 us (0.78)
  matrix products: 33.1 us -> 0 us
  local copies, waits for them, and re-layouts: 19.5 us -> 8.77 us
  other arithmetic: 4.85 us -> 0 us
  Pallas kernels: 146 us -> 150 us
    dot_general x14 -> x0, matrix products: 33.1 us -> none  [the longest x4 11.7 us: grad_rows(): jnp.einsum('ra,rb->ab', left, right, preferred_element_type=jnp.float32)]
    another operation x33 -> x0, local copies, waits for them, and re-layouts: 6.54 us -> none  [the longest x31 6.36 us: vector_rows(): return jnp.stack(rows, axis=1)]
    pallas_call x3 -> x1, Pallas kernels: 146 us -> 150 us  [fused(): pl.pallas_call(functools.partial(layer_kernel, tuple(named)), out_shape=[...]
    convert_element_type x2 -> x0, other arithmetic: 2.81 us -> none  [the longest x1 1.92 us: local(): gain_two.astype(fl)]
    unnamed x34 -> x16, local copies, waits for them, and re-layouts: 8.25 us -> 6.02 us
where the time goes in v1:
time: 160 us
  Pallas kernels  150 us (94%)
  local copies, waits for them, and re-layouts  8.77 us (5%)
    pallas_call x1, Pallas kernels, fused(): pl.pallas_call(functools.partial(layer_kernel, tuple(named)), out_shape=[...  150 us
    unnamed x16, local copies, waits for them, and re-layouts  6.02 us

profile of v1, /device:TPU:1, one launch (start us, length us, event | category | flops | bytes accessed | tf_op | source)
XLA Modules:
  0.0 159.6 jit_solution(11626312801820813602)
XLA Ops:
  0.7 150.1 %layer.1 = (bf16[128,768]{1,0:T(8,128)(2,1)}, f32[128,768]{1,0:T(8,128)}, f32[24,2304]{1,0:T(8,128)}, f32[24,768]{1,0:T(8,128)}, f32[24,3072]{1,0:T(8,128)}, /*index=5*/f32[96,768]{1,0:T(8,128)}, f32[16,128]{1,0:T(8,128)}) custom-call(bf16[128,768]{1,0:T(8,128)(2,1)} %refs_0_.1, s32[1,128]{1,0:T(1,128)} %bitcast.29, s32[1,128]{1,0:T(1,128)} %bitcast.30, ...), custom_call_target="tpu_custom_call" | custom-call | tf_op jit(solution)/shard_map/layer/pallas_call | solution.py:826
  150.8 0.0 copy-start
  150.8 1.2 slice_bitcast_fusion.3
  152.0 1.5 slice_bitcast_fusion
  153.5 1.6 %copy.38 = bf16[128,768]{1,0:T(8,128)(2,1)} copy(bf16[128,768]{1,0:T(8,128)(2,1)} %get-tuple-element.52) | data formatting | bytes 393216
  155.2 0.0 copy-done
  155.2 0.0 copy-start.3
  155.2 0.7 copy.39
  155.9 0.3 copy-done.3
  156.2 0.0 copy-start.4
  156.2 0.0 copy-start.2
  156.3 0.7 copy.40
  156.9 0.2 copy-done.4
  157.2 0.6 copy.41
  157.8 0.0 copy-done.2
  157.8 0.0 copy-start.1
  157.8 0.7 copy.42
  158.5 0.4 copy-done.1
  158.9 0.7 copy.43
Async XLA Ops:
  150.8 4.4 %copy-start = (f32[128,768]{1,0:T(8,128)S(1)}, f32[128,768]{1,0:T(8,128)}, u32[]{:S(2)}) copy-start(f32[128,768]{1,0:T(8,128)} %get-tuple-element.53) | copy-start | bytes 1179652
  155.2 1.1 copy-start.3
  156.2 0.9 copy-start.4
  156.2 1.5 copy-start.2
  157.8 1.1 copy-start.1

commit v2 on v1

--- a/solution.py
+++ b/solution.py
@@ -118,20 +118,39 @@
 
 X, Y, Z1, Z2 = 0, 1, 2, 3
 GATHER_ORDERS = (
+    (Z2, Z1, Y, X),
     (Z2, Z1, X, Y),
+    (Y, Z2, Z1, X),
     (Z2, Z1, Y, X),
-    (X, Z2, Z1, Y),
-    (Y, Z2, Z1, X),
-    (Z2, Z1, X, Y),
+    (Z2, Z1, Y),
+    (Z2, Z1, Y),
+    (Z2, Z1, Y, X),
 )
-SCATTER_ORDERS = tuple(tuple(reversed(o)) for o in GATHER_ORDERS)
+SCATTER_ORDERS = (
+    (X, Z1, Z2, Y),
+    (Y, X, Z1, Z2),
+    (X, Y, Z1, Z2),
+    (X, Y, Z1, Z2),
+    (Y, Z1, Z2),
+    (Y, Z1, Z2),
+    (Y, Z1, Z2, X),
+)
+GATHER_FIRST = (0, 0, 2, 2, 4, 5, 0)
+SCATTER_FIRST = (3, 0, 2, 1, 2, 3, 2)
+ADDS_BETWEEN = 2
+ADD_US = (0.15, 0.15, 0.15, 0.15, 0.3, 0.3, 0.08)
 PAIRS = 16
-PIECE_ROWS = (48, 48, 48, 192, 32)
-PIECE_COLS = (1152, 384, 1536, 384, 128)
-COUNT = 5
+PIECES = (16, 16, 16, 16, 8, 8, 16)
+PIECE_ROWS = (48, 48, 48, 48, 96, 192, 32)
+PIECE_COLS = (384, 384, 384, 384, 768, 384, 128)
+OUT, UP, DOWN, VEC = 3, 4, 5, 6
+QUAD = 4
+COUNT = 7
 HOPS = {X: ((0, 1),), Y: ((1, 1),), Z1: ((2, 1),), Z2: ((2, 1), (3, 2))}
 LINK_BYTES_PER_US = 46e3
 HOP_US = 1.0
+CORE_BYTES_PER_US = 600e3
+BACKLOG_US = 1.5
 FUSED_VMEM = 58 * 1024 * 1024
 
 
@@ -140,17 +159,38 @@
         self.now = 0.0
         self.free = {}
         self.pending = []
+        self.waiting = []
+        self.here = set()
         self.seq = 0
 
     def travel(self, dim, size, key):
-        us = size / LINK_BYTES_PER_US
-        begin = max([self.now] + [self.free.get(link, 0.0) for link, _ in HOPS[dim]])
+        if dim is None:
+            us, hops = size / CORE_BYTES_PER_US, ((4, 1),)
+        else:
+            us, hops = size / LINK_BYTES_PER_US, HOPS[dim]
+        begin = max([self.now] + [self.free.get(link, 0.0) for link, _ in hops])
         end = begin
-        for link, cost in HOPS[dim]:
+        for link, cost in hops:
             self.free[link] = begin + cost * us
             end = max(end, begin + cost * us)
+        self.seq += 1
         heapq.heappush(self.pending, (end + HOP_US, self.seq, key))
+
+    def ask(self, first, dim, size, key, start):
         self.seq += 1
+        self.waiting.append((first, self.seq, dim, size, key, start))
+        self.waiting.sort(key=lambda entry: entry[:2])
+
+    def pump(self):
+        left = []
+        for entry in self.waiting:
+            _, _, dim, size, key, start = entry
+            if max(self.free.get(link, 0.0) for link, _ in HOPS[dim]) - self.now < BACKLOG_US:
+                start()
+                self.travel(dim, size, key)
+            else:
+                left.append(entry)
+        self.waiting = left
 
 
 def subsets(order, step):
@@ -166,30 +206,38 @@
 
 ROWS_BOTH, COLS_BOTH = ((0,), (0,)), ((1,), (1,))
 
-SIBLING_COPIES = 25
+SIBLING_COPIES = 58
+INPUTS, OUTPUTS = 17, 7
+
+
+def stage_shape(k):
+    if k == UP:
+        return ((QUAD, 32, PIECE_COLS[k]), jnp.bfloat16)
+    return (((PIECE_ROWS[k] // 2 + 15) // 16 * 16, PIECE_COLS[k]), jnp.bfloat16)
 
 
 def scratch_of(rows, width, hidden):
     fl, bf = jnp.float32, jnp.bfloat16
-    both, half, hhalf = 2 * rows, width // 2, hidden // 2
+    both, half, quad = 2 * rows, width // 2, QUAD * rows
+    hhalf, hquarter = hidden // 2, hidden // 4
     lists = []
     for shape_of in (
-        lambda pr, pc: ((PAIRS * pr, pc), bf),
-        lambda pr, pc: ((PAIRS * pr, pc), bf),
-        lambda pr, pc: ((PAIRS - 1, pr, pc), bf),
-        lambda pr, pc: (((pr // 2 + 15) // 16 * 16, pc), bf),
-        lambda pr, pc: (((pr // 2 + 15) // 16 * 16, pc), bf),
-        lambda pr, pc: ((pr, pc), fl),
+        lambda k: ((PIECES[k] * PIECE_ROWS[k], PIECE_COLS[k]), bf),
+        lambda k: ((PIECES[k] * PIECE_ROWS[k], PIECE_COLS[k]), bf),
+        lambda k: ((PIECES[k] - 1, PIECE_ROWS[k], PIECE_COLS[k]), bf),
+        stage_shape,
+        stage_shape,
+        lambda k: ((PIECE_ROWS[k], PIECE_COLS[k]), fl),
     ):
-        lists += [shape_of(PIECE_ROWS[k], PIECE_COLS[k]) for k in range(COUNT)]
+        lists += [shape_of(k) for k in range(COUNT)]
     named = dict(
-        peer_part4=((PAIRS * PIECE_ROWS[4], PIECE_COLS[4]), bf),
-        stage_part4=((PAIRS * PIECE_ROWS[4], PIECE_COLS[4]), bf),
+        peer_vec=((PAIRS * PIECE_ROWS[VEC], PIECE_COLS[VEC]), bf),
+        stage_vec=((PAIRS * PIECE_ROWS[VEC], PIECE_COLS[VEC]), bf),
         tok=((both, width), bf),
         marks=((2, 8, rows), fl),
         vec32=((PAIRS * 32, 128), fl),
         vecs=((16, width), fl),
-        upb=((8, hhalf), fl),
+        upb=((8, hquarter), fl),
         qkv=((both, 3 * half), bf),
         probs=((HEADS, rows, rows), fl),
         ctx=((both, width), bf),
@@ -199,21 +247,25 @@
         hid=((rows, width), fl),
         n1=((rows, width), fl),
         i1=((rows, 128), fl),
-        hb=((both, width), bf),
-        act=((both, hidden), bf),
-        fac=((both, hhalf), fl),
+        hb=((quad, width), bf),
+        act=((quad, hhalf), bf),
+        fac=((quad, hquarter), fl),
         ffn_s=((rows, half), fl),
         ffn_r=((rows, half), fl),
-        ffn_o=((rows, half), fl),
+        ffn_o=((both, half), fl),
+        ffn_xs=((both, half), bf),
+        ffn_xr=((both, half), bf),
         dff=((rows, width), fl),
-        dfb=((both, width), bf),
-        dact_s=((both, hhalf), fl),
-        dact_r=((both, hhalf), fl),
-        dact_o=((both, hhalf), fl),
-        dpre=((both, hhalf), bf),
-        dhid_s=((rows, width), fl),
-        dhid_r=((rows, width), fl),
-        dhid_o=((rows, width), fl),
+        dfb=((quad, width), bf),
+        dact_s=((quad, hquarter), fl),
+        dact_r=((quad, hquarter), fl),
+        dact_o=((quad, hquarter), fl),
+        dpre=((quad, hquarter), bf),
+        dhid_s=((both, width), fl),
+        dhid_r=((both, width), fl),
+        dhid_o=((both, width), fl),
+        dhid_xs=((rows, width), bf),
+        dhid_xr=((rows, width), bf),
         dat=((rows, width), fl),
         datb=((both, width), bf),
         dctx_s=((both, half), fl),
@@ -225,7 +277,9 @@
         tg_r=((rows, width), fl),
         tg_o=((rows, width), fl),
         sums=((16, width), fl),
-        upsum=((8, hhalf), fl),
+        upsum=((8, hquarter), fl),
+        mixed=((width // GROUP, hidden), fl),
+        mixed_qkv=((width // GROUP, 3 * width), fl),
     )
     return lists, named
 
@@ -238,17 +292,28 @@
         return taken
 
     R = types.SimpleNamespace()
-    R.tokens, R.doc, R.pad = take(3)
-    R.w, R.v, R.cotangent = take(4), take(9), take(1)[0]
-    R.layer_out, R.token_grad = take(2)
-    R.g, R.gv = take(4), take(1)[0]
+    far_in, far_out, near_in, near_out = take(INPUTS), take(OUTPUTS), take(INPUTS), take(OUTPUTS)
+    R.tokens, R.doc, R.pad, R.cotangent = near_in[:4]
+    R.w, R.v = near_in[4:8], near_in[8:]
+    R.layer_out, R.token_grad, R.gv = near_out[:3]
+    R.g = near_out[3:]
     R.whole, R.part, R.land, R.stage, R.peer, R.fin = (take(COUNT) for _ in range(6))
     vars(R).update(zip(names, take(len(names))))
-    sib_send, sib_recv, g_send, g_recv, s_send, s_recv = refs
+    sib_send, sib_recv, g_send, g_recv, s_send, s_recv, in_sem, out_sem = refs
+    loads = [
+        pltpu.make_async_copy(far, near, in_sem.at[i])
+        for i, (far, near) in enumerate(zip(far_in, near_in))
+    ]
+    for i in (4, *range(8, 17), 5, 6, 7, 0, 1, 2, 3):
+        loads[i].start()
+    stores = [
+        pltpu.make_async_copy(near, far, out_sem.at[i])
+        for i, (far, near) in enumerate(zip(far_out, near_out))
+    ]
     fl, bf = jnp.float32, jnp.bfloat16
     rows, width = R.tokens.shape
     hidden = R.w[2].shape[1]
-    half, hhalf = width // 2, hidden // 2
+    half, hhalf, hquarter = width // 2, hidden // 2, hidden // 4
     size = width // HEADS
     scale = 1.0 / math.sqrt(size)
     me = lax.axis_index(AXIS)
@@ -265,6 +330,13 @@
                 p = p + (1 << b) * (1 - 2 * bits[b])
         return p
 
+    def quad_of(r):
+        q = lax.div(pair, 2)
+        for b in range(1, 4):
+            if r >> b & 1:
+                q = q + (1 << (b - 1)) * (1 - 2 * bits[b])
+        return q
+
     def device_along(b):
         return me + (2 << b) * (1 - 2 * bits[b])
 
@@ -274,28 +346,45 @@
 
     own_rows, sib_rows = pl.ds(by_core(rows), rows), pl.ds(by_core(rows, 1), rows)
     own_half, sib_half = pl.ds(by_core(half), half), pl.ds(by_core(half, 1), half)
-    own_hh, sib_hh = pl.ds(by_core(hhalf), hhalf), pl.ds(by_core(hhalf, 1), hhalf)
+    own_hq, sib_hq = pl.ds(by_core(hquarter), hquarter), pl.ds(by_core(hquarter, 1), hquarter)
+    x_at = bits[X]
+    across = device_along(X)
+    diagonal = across + 1 - 2 * core
+    member = 2 * x_at + core
+
+    def quad_rows(other_x, other_core, count=rows, skip=0):
+        at = 2 * (1 - x_at if other_x else x_at) + (1 - core if other_core else core)
+        return pl.ds(pl.multiple_of(at * rows + skip, 64), count)
+
+    def chip_rows(other_x):
+        return pl.ds(pl.multiple_of((1 - x_at if other_x else x_at) * 2 * rows, 128), 2 * rows)
+
 
     barrier = pltpu.get_barrier_semaphore()
-    for other in [sibling] + [device_along(b) for b in range(4)]:
+    for other in [sibling, diagonal] + [device_along(b) for b in range(4)]:
         pl.semaphore_signal(barrier, inc=1, device_id=(other,), device_id_type=MESH_IDS)
-    pl.semaphore_wait(barrier, 5)
-
+    pl.semaphore_wait(barrier, 6)
+
+    plan = Plan()
     sib = {}
     sent = []
 
-    def to_sibling(i, src, dst):
+    def to_sibling(i, src, dst, device=None):
         copy = pltpu.make_async_remote_copy(
             src_ref=src,
             dst_ref=dst,
             send_sem=sib_send.at[i],
             recv_sem=sib_recv.at[i],
-            device_id=(sibling,),
+            device_id=(sibling if device is None else device,),
             device_id_type=MESH_IDS,
         )
         copy.start()
         sib[i] = copy
         sent.append(copy)
+        plan.travel(None if device is None else X, math.prod(src.shape) * src.dtype.itemsize, (None, i))
+
+    def arrived(i):
+        sib.pop(i).wait_recv()
 
     def side_by_side(own, other):
         return jnp.concatenate(
@@ -303,14 +392,15 @@
         )
 
     def shard_half(k, mine):
-        ref = R.w[k]
-        if k == 0:
+        which = core if mine else 1 - core
+        if k < 3:
             cols = [
-                ref[:, pl.ds(pl.multiple_of(p * width + (core if mine else 1 - core) * half, 128), half)]
+                R.w[0][:, pl.ds(pl.multiple_of(p * width + which * half + k * 128, 128), 128)]
                 for p in range(3)
             ]
             return jnp.concatenate([c.astype(fl) for c in cols], axis=1)
         cols = PIECE_COLS[k]
+        ref = R.w[1] if k == OUT else R.w[3]
         return ref[:, pl.ds(by_core(cols, None if mine else 1), cols)].astype(fl)
 
     def padded(value):
@@ -319,16 +409,34 @@
             value = jnp.concatenate([value, jnp.zeros((short, value.shape[1]), fl)], axis=0)
         return value.astype(bf)
 
-    R.stage[4][...] = jnp.zeros(R.stage[4].shape, bf)
+    for load in loads[4:]:
+        load.wait()
     R.vec32[pl.ds(0, 16), :] = jnp.zeros((16, 128), fl)
     for j in range(9):
         v = R.v[j]
         R.vec32[j : j + 1, 0 : v.shape[1]] = v[...].astype(fl)
-    R.stage[4][...] = R.vec32[pl.ds(0, 16), :].astype(bf)
-    for k in (0, 4, 1, 2, 3):
-        if k < 4:
+    R.stage[VEC][...] = R.vec32[pl.ds(0, 16), :].astype(bf)
+    def quarter(q):
+        blocks = []
+        for j in range(4):
+            at = (q % 2) * hhalf + 2 * j * 192 + (q // 2) * 192
+            blocks.append(R.w[2][:, at : at + 192].astype(fl))
+        return jnp.concatenate(blocks, axis=1)
+
+    for k in (0, VEC, 1, 2, OUT, DOWN):
+        if k != VEC:
             R.stage[k][...] = padded(shard_half(k, False))
-        to_sibling(k, R.stage[k], R.peer[k])
+        to_sibling(50 + k, R.stage[k], R.peer[k])
+    for q in range(QUAD):
+        R.stage[UP][q] = padded(quarter(q))
+    for i, device, q in (
+        (54, None, member + 1 - 2 * core),
+        (25, across, member + 2 - 4 * x_at),
+        (26, diagonal, 3 - member),
+    ):
+        to_sibling(i, R.stage[UP].at[q], R.peer[UP].at[member], device)
+    for load in loads[:4]:
+        load.wait()
     to_sibling(5, R.tokens, R.tok.at[own_rows])
     own_marks = jnp.concatenate(
         [R.doc[...].astype(fl), R.pad[...].astype(fl), jnp.zeros((6, rows), fl)], axis=0
@@ -337,13 +445,14 @@
     to_sibling(6, R.marks.at[core], R.marks.at[core])
     R.tok[own_rows, :] = R.tokens[...]
 
-    plan = Plan()
+    plan.now = 3.0
     piece_bytes = [2 * PIECE_ROWS[k] * PIECE_COLS[k] for k in range(COUNT)]
     done = [1] * COUNT
 
     def piece_at(k, r):
         n = PIECE_ROWS[k]
-        return pl.ds(pl.multiple_of(pair_of(r) * n, n), n)
+        place = pair_of(r) if PIECES[k] == PAIRS else quad_of(r)
+        return pl.ds(pl.multiple_of(place * n, n), n)
 
     def gather_move(k, r, b):
         at = piece_at(k, r)
@@ -356,22 +465,24 @@
             device_id=(device_along(b),),
             device_id_type=MESH_IDS,
         )
-        copy.start()
         sent.append(copy)
-        plan.travel(b, piece_bytes[k], (True, k, slot, b))
-
-    for k in (0, 4, 1, 2, 3):
-        sib[k].wait_recv()
-        if k < 4:
-            mine = shard_half(k, True)
+        plan.ask(GATHER_FIRST[k], b, piece_bytes[k], (True, k, slot, b), copy.start)
+
+    for k in (0, VEC, 1, 2, OUT, DOWN, UP):
+        arrived(50 + k)
+        if k == UP:
+            R.peer[UP][member] = R.stage[UP][member]
+            arrived(25)
+            arrived(26)
+            rows_in = [R.peer[UP][q].astype(fl)[: width // GROUP] for q in range(QUAD)]
         else:
-            mine = R.vec32[pl.ds(0, 16), :]
-        theirs = R.peer[k][...].astype(fl)[: mine.shape[0]]
-        R.whole[k][piece_at(k, 0), :] = jnp.concatenate(
-            [jnp.where(is_first, mine, theirs), jnp.where(is_first, theirs, mine)], axis=0
-        ).astype(bf)
+            mine = R.vec32[pl.ds(0, 16), :] if k == VEC else shard_half(k, True)
+            theirs = R.peer[k][...].astype(fl)[: mine.shape[0]]
+            rows_in = [jnp.where(is_first, mine, theirs), jnp.where(is_first, theirs, mine)]
+        R.whole[k][piece_at(k, 0), :] = jnp.concatenate(rows_in, axis=0).astype(bf)
         for b in GATHER_ORDERS[k]:
             gather_move(k, 0, b)
+        plan.pump()
 
     def on_gather(k, r, b):
         here = R.whole[k].at[piece_at(k, r)]
@@ -391,7 +502,7 @@
     slot_of = []
     for k in range(COUNT):
         table = {}
-        for step in range(4):
+        for step in range(len(SCATTER_ORDERS[k])):
             for r in subsets(SCATTER_ORDERS[k], step):
                 table[step, r] = len(table)
         slot_of.append(table)
@@ -414,10 +525,9 @@
             device_id=(device_along(b),),
             device_id_type=MESH_IDS,
         )
-        copy.start()
         sent.append(copy)
         copies[k, step, low] = copy
-        plan.travel(b, piece_bytes[k], (False, k, step, low))
+        plan.ask(SCATTER_FIRST[k], b, piece_bytes[k], (False, k, step, low), copy.start)
 
     def scatter_start(k):
         order = SCATTER_ORDERS[k]
@@ -425,22 +535,34 @@
             scatter_move(k, 0, r | (1 << order[0]))
 
     def finish(k):
-        if k == 4:
-            R.gv[...] = R.fin[4][pl.ds(by_core(16), 16), :]
+        if k == VEC:
+            R.gv[...] = R.fin[VEC][pl.ds(by_core(16), 16), :]
+            stores[2].start()
+            return
+        if k == UP:
+            at = pl.ds(pl.multiple_of(x_at * hhalf + core * hquarter, 128), hquarter)
+            n = PIECE_ROWS[UP] // QUAD
+
+            def share(q):
+                return R.fin[UP].at[pl.ds(pl.multiple_of(q * n, n), n)]
+
+            for i, device, q in (
+                (22, None, member + 1 - 2 * core),
+                (27, across, member + 2 - 4 * x_at),
+                (28, diagonal, 3 - member),
+            ):
+                to_sibling(i, share(q), R.mixed.at[:, at], device)
+            R.mixed[:, at] = share(member)[...]
             return
         n = PIECE_ROWS[k] // 2
         mine = R.fin[k].at[pl.ds(by_core(n), n)]
         theirs = R.fin[k].at[pl.ds(by_core(n, 1), n)]
-        if k == 0:
-            for p in range(3):
-                at = pl.ds(pl.multiple_of(p * width + core * half, 128), half)
-                part = pl.ds(p * half, half)
-                to_sibling(18 + p, theirs.at[:, part], R.g[0].at[:, at])
-                R.g[0][:, at] = mine[:, part]
+        if k < 3:
+            into, at = R.mixed_qkv, pl.ds(pl.multiple_of((3 * core + k) * 384, 384), 384)
         else:
-            at = pl.ds(by_core(PIECE_COLS[k]), PIECE_COLS[k])
-            to_sibling(20 + k, theirs, R.g[k].at[:, at])
-            R.g[k][:, at] = mine[...]
+            into, at = R.g[1 if k == OUT else 3], own_half
+        to_sibling(18 + k, theirs, into.at[:, at])
+        into[:, at] = mine[...]
 
     summed = set()
     early = {}
@@ -450,6 +572,7 @@
             early[k, step - 1, r] = step
             return
         summed.add((k, step, r))
+        plan.now += ADD_US[k]
         add_piece(k, step, r)
         if (k, step, r) in early:
             on_scatter(k, early[k, step, r], r)
@@ -459,7 +582,7 @@
         order = SCATTER_ORDERS[k]
         before, now = held(k, step - 1, r), held(k, step, r)
         total = now[...].astype(fl) + before[...].astype(fl)
-        if step == 3:
+        if step == len(order) - 1:
             R.fin[k][...] = total
             finish(k)
             return
@@ -475,19 +598,24 @@
         i = lax.broadcasted_iota(jnp.int32, (128, count), 0).astype(fl)
         return jnp.where(n - period * column_of(n, period) == i, 1.0, 0.0).astype(bf)
 
-    def owner_is(count, period, first):
+    def owner_is(count, period):
         n = lax.broadcasted_iota(jnp.int32, (GROUP, count), 1).astype(fl)
         d = lax.broadcasted_iota(jnp.int32, (GROUP, count), 0).astype(fl)
-        return column_of(n, period) + first == d
+        return column_of(n, period) == d
 
     small, large = width // GROUP, hidden // GROUP
 
-    def half_first():
-        return jnp.where(is_first, 0.0, GROUP / 2.0)
+    def unit_owner():
+        n = lax.broadcasted_iota(jnp.int32, (GROUP, hquarter), 1).astype(fl)
+        d = lax.broadcasted_iota(jnp.int32, (GROUP, hquarter), 0).astype(fl)
+        block = column_of(n, large)
+        quad = column_of(block, 2)
+        first = (16 * core + 2 * x_at).astype(fl)
+        return first + 4.0 * quad + (block - 2.0 * quad) == d
 
     def task_vectors():
-        R.vec32[...] = R.whole[4][...].astype(fl)
-        chosen, owner = pick(width, small), owner_is(width, small, 0.0)
+        R.vec32[...] = R.whole[VEC][...].astype(fl)
+        chosen, owner = pick(width, small), owner_is(width, small)
         for j in range(8):
             v = R.vec32[pl.ds(j, GROUP, stride=16), :].astype(bf)
             R.vecs[j : j + 1, :] = jnp.sum(
@@ -495,7 +623,7 @@
             )
         v = R.vec32[pl.ds(8, GROUP, stride=16), :].astype(bf)
         R.upb[0:1, :] = jnp.sum(
-            jnp.where(owner_is(hhalf, large, half_first()), dot(v, pick(hhalf, large)), 0.0),
+            jnp.where(unit_owner(), dot(v, pick(hquarter, large)), 0.0),
             axis=0,
             keepdims=True,
         )
@@ -503,15 +631,17 @@
     def vec(j):
         return R.vecs[j : j + 1, :]
 
-    def task_qkv():
-        sib[5].wait_recv()
-        sib[6].wait_recv()
+    def task_qkv(two):
+        if two == 0:
+            arrived(5)
+            arrived(6)
+        value = dot(R.tok[...], R.whole[two][...])
         for p in range(3):
-            at = pl.ds(p * half, half)
-            value = dot(R.tok[...], R.whole[0][:, at])
+            block = value[:, p * 128 : (p + 1) * 128]
             if p != 1:
-                value = value + R.vecs[p // 2 : p // 2 + 1, own_half]
-            R.qkv[:, at] = value.astype(bf)
+                at = pl.ds(pl.multiple_of(core * half + two * 128, 128), 128)
+                block = block + R.vecs[p // 2 : p // 2 + 1, at]
+            R.qkv[:, two * 384 + p * 128 : two * 384 + (p + 1) * 128] = block.astype(bf)
 
     def seen(b):
         doc, pad = R.marks[b, 0:1, :], R.marks[b, 1:2, :]
@@ -524,9 +654,9 @@
 
     def head_of(b, h):
         at = b * rows
+        first = h // 2 * 384 + h % 2 * size
         return [
-            R.qkv[at : at + rows, p * half + h * size : p * half + (h + 1) * size]
-            for p in range(3)
+            R.qkv[at : at + rows, first + p * 128 : first + p * 128 + size] for p in range(3)
         ]
 
     def task_attention(b, two):
@@ -542,14 +672,16 @@
             found.append(dot(probs.astype(bf), value_rows))
         at = pl.ds(pl.multiple_of(core * half + two * 2 * size, 128), 2 * size)
         R.ctx[pl.ds(b * rows, rows), at] = jnp.concatenate(found, axis=1).astype(bf)
-        if b == 1 and two == HEADS // 4 - 1:
-            to_sibling(7, R.ctx.at[:, own_half], R.ctx.at[:, own_half])
+        if b == 1:
+            to_sibling((7, 45, 46)[two], R.ctx.at[:, at], R.ctx.at[:, at])
 
     def task_project():
-        sib[7].wait_recv()
-        R.proj_s[...] = dot(R.ctx[sib_rows, :], R.whole[1][...])
+        arrived(7)
+        arrived(45)
+        arrived(46)
+        R.proj_s[...] = dot(R.ctx[sib_rows, :], R.whole[OUT][...])
         to_sibling(8, R.proj_s, R.proj_r)
-        R.proj_o[...] = dot(R.ctx[own_rows, :], R.whole[1][...])
+        R.proj_o[...] = dot(R.ctx[own_rows, :], R.whole[OUT][...])
 
     def norm(values):
         centred = values - jnp.mean(values, axis=-1, keepdims=True)
@@ -557,7 +689,7 @@
         return centred * inverse, inverse
 
     def task_norm_one():
-        sib[8].wait_recv()
+        arrived(8)
         attn = (
             R.tokens[...].astype(fl)
             + side_by_side(R.proj_o[...], R.proj_r[...])
@@ -568,33 +700,60 @@
         R.n1[...] = normed
         R.i1[...] = jnp.broadcast_to(inverse, (rows, 128))
         R.hid[...] = hid
-        R.hb[own_rows, :] = hid.astype(bf)
-        to_sibling(9, R.hb.at[own_rows], R.hb.at[own_rows])
+        R.hb[quad_rows(0, 0), :] = hid.astype(bf)
+        spread_rows(R.hb, 9, 29)
 
     tile = 384
 
-    def task_up():
-        sib[9].wait_recv()
+    def spread_rows(ref, i, first):
+        for skip in (0, 1):
+            at = quad_rows(0, 0, rows // 2, skip * (rows // 2))
+            to_sibling(first + skip, ref.at[at], ref.at[at], across)
+        at = quad_rows(0, 0)
+        to_sibling(i, ref.at[at], ref.at[at])
+
+    def pass_on(ref, first):
+        for skip in (0, 1):
+            arrived(first + skip)
+            at = quad_rows(1, 0, rows // 2, skip * (rows // 2))
+            to_sibling(first + 2 + skip, ref.at[at], ref.at[at])
+
+    def task_up(other):
+        if other:
+            arrived(31)
+            arrived(32)
+        else:
+            arrived(9)
+        to = chip_rows(other)
 
         def body(t, carry):
             at = pl.ds(pl.multiple_of(t * tile, tile), tile)
-            pre = dot(R.hb[...], R.whole[2][:, at]) + R.upb[0:1, at]
+            pre = dot(R.hb[to, :], R.whole[UP][:, at]) + R.upb[0:1, at]
             cdf = 0.5 * (1.0 + lax.erf(pre * root_half))
             pdf = jnp.exp(-0.5 * pre * pre) * inv_root_two_pi
-            R.fac[:, at] = cdf + pre * pdf
-            R.act[:, pl.ds(pl.multiple_of(core * hhalf + t * tile, tile), tile)] = (
+            R.fac[to, at] = cdf + pre * pdf
+            R.act[to, pl.ds(pl.multiple_of(core * hquarter + t * tile, tile), tile)] = (
                 pre * cdf
             ).astype(bf)
             return carry
 
-        lax.fori_loop(0, hhalf // tile, body, 0)
-        to_sibling(10, R.act.at[:, own_hh], R.act.at[:, own_hh])
+        lax.fori_loop(0, hquarter // tile, body, 0)
+        to_sibling(33 + other, R.act.at[to, own_hq], R.act.at[to, own_hq])
 
     def task_ffn():
-        sib[10].wait_recv()
-        R.ffn_s[...] = dot(R.act[sib_rows, :], R.whole[3][...])
+        arrived(33)
+        arrived(34)
+        for i, other_core in ((35, 1), (36, 0)):
+            at = pl.ds(by_core(rows, 1 if other_core else None), rows)
+            R.ffn_xs[at, :] = dot(R.act[quad_rows(1, other_core), :], R.whole[DOWN][...]).astype(bf)
+            to_sibling(i, R.ffn_xs.at[at], R.ffn_xr.at[at], across)
+        R.ffn_o[...] = dot(R.act[chip_rows(0), :], R.whole[DOWN][...])
+
+    def task_ffn_sum():
+        arrived(35)
+        R.ffn_s[...] = R.ffn_o[sib_rows, :] + R.ffn_xr[sib_rows, :].astype(fl)
         to_sibling(11, R.ffn_s, R.ffn_r)
-        R.ffn_o[...] = dot(R.act[own_rows, :], R.whole[3][...])
+        arrived(36)
 
     def back_of_norm(upstream, normed, inverse, gain):
         scaled = upstream * gain
@@ -608,46 +767,45 @@
         R.sums[j : j + 1, :] = jnp.sum(values, axis=0, keepdims=True)
 
     def task_norm_two():
-        sib[11].wait_recv()
-        total = R.hid[...] + side_by_side(R.ffn_o[...], R.ffn_r[...]) + vec(5)
+        arrived(11)
+        mine = R.ffn_o[own_rows, :] + R.ffn_xr[own_rows, :].astype(fl)
+        total = R.hid[...] + side_by_side(mine, R.ffn_r[...]) + vec(5)
         normed, inverse = norm(total)
         R.layer_out[...] = (normed * vec(6) + vec(7)).astype(bf)
+        stores[0].start()
         upstream = R.cotangent[...].astype(fl)
         d_ffn = back_of_norm(upstream, normed, inverse, vec(6))
         R.dff[...] = d_ffn
-        R.dfb[own_rows, :] = d_ffn.astype(bf)
-        to_sibling(12, R.dfb.at[own_rows], R.dfb.at[own_rows])
+        R.dfb[quad_rows(0, 0), :] = d_ffn.astype(bf)
+        spread_rows(R.dfb, 12, 37)
         add_sum(6, upstream * normed)
         add_sum(7, upstream)
         add_sum(5, d_ffn)
 
     def task_grad_down():
-        sib[12].wait_recv()
+        arrived(39)
+        arrived(40)
 
         def body(t, carry):
             at = pl.ds(pl.multiple_of(t * tile, tile), tile)
-            R.part[3][at, :] = dot(R.act[:, at], R.dfb[:, own_half], ROWS_BOTH).astype(bf)
+            R.part[DOWN][at, :] = dot(R.act[:, at], R.dfb[:, own_half], ROWS_BOTH).astype(bf)
             return carry
 
-        lax.fori_loop(0, hidden // tile, body, 0)
-        scatter_start(3)
-
-    def d_act_half(which, into):
-        def body(t, carry):
-            src = pl.ds(pl.multiple_of(which * hhalf + t * tile, tile), tile)
-            at = pl.ds(pl.multiple_of(t * tile, tile), tile)
-            into[:, at] = dot(R.dfb[:, own_half], R.whole[3][src, :], COLS_BOTH)
-            return carry
-
         lax.fori_loop(0, hhalf // tile, body, 0)
-
-    def task_d_act():
-        d_act_half(1 - core, R.dact_s)
-        to_sibling(13, R.dact_s, R.dact_r)
-        d_act_half(core, R.dact_o)
+        scatter_start(DOWN)
+
+    def task_d_act(other):
+        if not other:
+            arrived(12)
+        at = chip_rows(other)
+        right = R.dfb[at, own_half]
+        R.dact_s[at, :] = dot(right, R.whole[DOWN][sib_hq, :], COLS_BOTH)
+        to_sibling(41 + other, R.dact_s.at[at], R.dact_r.at[at])
+        R.dact_o[at, :] = dot(right, R.whole[DOWN][own_hq, :], COLS_BOTH)
 
     def task_d_pre():
-        sib[13].wait_recv()
+        arrived(41)
+        arrived(42)
 
         def body(t, carry):
             at = pl.ds(pl.multiple_of(t * tile, tile), tile)
@@ -656,25 +814,38 @@
             R.dpre[:, at] = value.astype(bf)
             return carry
 
-        lax.fori_loop(0, hhalf // tile, body, 0)
+        lax.fori_loop(0, hquarter // tile, body, 0)
 
     def task_d_hidden():
-        R.dhid_s[...] = dot(R.dpre[sib_rows, :], R.whole[2][...], COLS_BOTH)
-        to_sibling(14, R.dhid_s, R.dhid_r)
-        R.dhid_o[...] = dot(R.dpre[own_rows, :], R.whole[2][...], COLS_BOTH)
+        for i, other_x in ((14, 1), (43, 0)):
+            at = pl.ds(other_x * rows, rows)
+            R.dhid_s[at, :] = dot(R.dpre[quad_rows(other_x, 1), :], R.whole[UP][...], COLS_BOTH)
+            to_sibling(i, R.dhid_s.at[at], R.dhid_r.at[at])
+        for other_x in (1, 0):
+            R.dhid_o[pl.ds(other_x * rows, rows), :] = dot(
+                R.dpre[quad_rows(other_x, 0), :], R.whole[UP][...], COLS_BOTH
+            )
+
+    def task_d_hidden_sum():
+        arrived(14)
+        at = pl.ds(rows, rows)
+        R.dhid_xs[...] = (R.dhid_o[at, :] + R.dhid_r[at, :]).astype(bf)
+        to_sibling(44, R.dhid_xs, R.dhid_xr, across)
 
     def task_grad_up():
         def body(t, carry):
             at = pl.ds(pl.multiple_of(t * tile, tile), tile)
-            R.part[2][:, at] = dot(R.hb[...], R.dpre[:, at], ROWS_BOTH).astype(bf)
+            R.part[UP][:, at] = dot(R.hb[...], R.dpre[:, at], ROWS_BOTH).astype(bf)
             return carry
 
-        lax.fori_loop(0, hhalf // tile, body, 0)
-        scatter_start(2)
+        lax.fori_loop(0, hquarter // tile, body, 0)
+        scatter_start(UP)
 
     def task_norm_one_back():
-        sib[14].wait_recv()
-        d_hid = R.dff[...] + R.dhid_o[...] + R.dhid_r[...]
+        arrived(43)
+        arrived(44)
+        at = pl.ds(0, rows)
+        d_hid = R.dff[...] + R.dhid_o[at, :] + R.dhid_r[at, :] + R.dhid_xr[...].astype(fl)
         normed = R.n1[...]
         d_attn = back_of_norm(d_hid, normed, R.i1[:, 0:1], vec(3))
         R.dat[...] = d_attn
@@ -685,18 +856,18 @@
         add_sum(2, d_attn)
 
     def task_d_context():
-        sib[15].wait_recv()
+        arrived(15)
         right = R.datb[:, own_half]
-        R.dctx_s[...] = dot(right, R.whole[1][sib_half, :], COLS_BOTH)
+        R.dctx_s[...] = dot(right, R.whole[OUT][sib_half, :], COLS_BOTH)
         to_sibling(16, R.dctx_s, R.dctx_r)
-        R.dctx_o[...] = dot(right, R.whole[1][own_half, :], COLS_BOTH)
+        R.dctx_o[...] = dot(right, R.whole[OUT][own_half, :], COLS_BOTH)
 
     def task_grad_out():
-        R.part[1][...] = dot(R.ctx[...], R.datb[:, own_half], ROWS_BOTH).astype(bf)
-        scatter_start(1)
+        R.part[OUT][...] = dot(R.ctx[...], R.datb[:, own_half], ROWS_BOTH).astype(bf)
+        scatter_start(OUT)
 
     def task_d_context_sum():
-        sib[16].wait_recv()
+        arrived(16)
         R.dctx[...] = (R.dctx_o[...] + R.dctx_r[...]).astype(bf)
 
     bias_sums = {}
@@ -715,7 +886,7 @@
             found.append((dot(d_scores, key_rows), dot(d_scores, query, ROWS_BOTH), d_value))
         for p in range(3):
             block = jnp.concatenate([found[0][p], found[1][p]], axis=1)
-            cols = p * half + two * 2 * size
+            cols = two * 384 + p * 128
             R.dqkv[at : at + rows, cols : cols + 2 * size] = block.astype(bf)
             if p != 1:
                 total = jnp.sum(block, axis=0, keepdims=True)
@@ -728,86 +899,151 @@
     def task_clear_sums():
         R.sums[...] = jnp.zeros(R.sums.shape, fl)
 
-    def task_grad_qkv():
-        for p in range(3):
-            at = pl.ds(p * half, half)
-            R.part[0][:, at] = dot(R.tok[...], R.dqkv[:, at], ROWS_BOTH).astype(bf)
-        scatter_start(0)
+    def task_grad_qkv(two):
+        at = pl.ds(two * 384, 384)
+        R.part[two][...] = dot(R.tok[...], R.dqkv[:, at], ROWS_BOTH).astype(bf)
+        scatter_start(two)
+
+    def through_qkv(at):
+        return sum(
+            dot(R.dqkv[at, pl.ds(two * 384, 384)], R.whole[two][...], COLS_BOTH)
+            for two in range(3)
+        )
 
     def task_token_grad():
-        R.tg_s[...] = dot(R.dqkv[sib_rows, :], R.whole[0][...], COLS_BOTH)
+        R.tg_s[...] = through_qkv(sib_rows)
         to_sibling(17, R.tg_s, R.tg_r)
-        R.tg_o[...] = R.dat[...] + dot(R.dqkv[own_rows, :], R.whole[0][...], COLS_BOTH)
+        R.tg_o[...] = R.dat[...] + through_qkv(own_rows)
 
     def task_sums():
-        chosen, owner = pick(width, small), owner_is(width, small, 0.0)
+        chosen, owner = pick(width, small), owner_is(width, small)
         R.vec32[...] = jnp.zeros(R.vec32.shape, fl)
         for j in range(8):
             spread = jnp.where(owner, R.sums[j : j + 1, :], 0.0).astype(bf)
             R.vec32[pl.ds(j, GROUP, stride=16), :] = dot(spread, chosen, COLS_BOTH)
-        spread = jnp.where(
-            owner_is(hhalf, large, half_first()), R.upsum[0:1, :], 0.0
-        ).astype(bf)
-        R.vec32[pl.ds(8, GROUP, stride=16), :] = dot(spread, pick(hhalf, large), COLS_BOTH)
-        R.stage_part4[...] = R.vec32[...].astype(bf)
-        to_sibling(24, R.stage_part4, R.peer_part4)
+        spread = jnp.where(unit_owner(), R.upsum[0:1, :], 0.0).astype(bf)
+        R.vec32[pl.ds(8, GROUP, stride=16), :] = dot(spread, pick(hquarter, large), COLS_BOTH)
+        R.stage_vec[...] = R.vec32[...].astype(bf)
+        to_sibling(24, R.stage_vec, R.peer_vec)
 
     def task_sums_send():
-        sib[24].wait_recv()
-        R.part[4][...] = (R.vec32[...] + R.peer_part4[...].astype(fl)).astype(bf)
-        scatter_start(4)
+        arrived(24)
+        R.part[VEC][...] = (R.vec32[...] + R.peer_vec[...].astype(fl)).astype(bf)
+        scatter_start(VEC)
 
     def task_token_grad_sum():
-        sib[17].wait_recv()
+        arrived(17)
         R.token_grad[...] = R.tg_o[...] + R.tg_r[...]
-
-    two_heads = [(b, two) for b in range(2) for two in range(HEADS // 4)]
-    tasks = [(task_clear_sums, (), 0.1), (task_vectors, (4,), 0.8), (task_qkv, (0,), 1.2)]
-    tasks += [(functools.partial(task_attention, b, two), (), 1.0) for b, two in two_heads]
+        stores[1].start()
+
+    call = functools.partial
+    tasks = [(task_clear_sums, (), (), 0.1), (task_vectors, (VEC,), (), 0.6)]
+    for two in range(3):
+        tasks += [(call(task_qkv, two), (two,), (5, 6), 0.4)]
+        tasks += [(call(task_attention, b, two), (), (), 0.9) for b in range(2)]
     tasks += [
-        (task_project, (1,), 1.5),
-        (task_norm_one, (), 1.5),
-        (task_up, (2,), 5.0),
-        (task_ffn, (3,), 1.5),
-        (task_norm_two, (), 2.0),
-        (task_grad_down, (), 2.5),
-        (task_d_act, (), 1.5),
-        (task_d_pre, (), 1.5),
-        (task_d_hidden, (), 1.0),
-        (task_grad_up, (), 1.5),
-        (task_norm_one_back, (), 1.0),
-        (task_d_context, (), 1.5),
-        (task_grad_out, (), 0.7),
-        (task_d_context_sum, (), 0.5),
+        (task_project, (OUT,), (7, 45, 46), 1.0),
+        (task_norm_one, (), (8,), 1.0),
+        (call(task_up, 0), (UP,), (9,), 1.8),
+        (call(pass_on, R.hb, 29), (), (29, 30), 0.2),
+        (call(task_up, 1), (), (31, 32), 1.8),
+        (task_ffn, (DOWN,), (33, 34), 1.5),
+        (task_ffn_sum, (), (35, 36), 0.4),
+        (task_norm_two, (), (11,), 1.2),
+        (call(task_d_act, 0), (), (12,), 1.2),
+        (call(pass_on, R.dfb, 37), (), (37, 38), 0.2),
+        (task_grad_down, (), (39, 40), 1.7),
+        (call(task_d_act, 1), (), (), 1.2),
+        (task_d_pre, (), (41, 42), 0.6),
+        (task_d_hidden, (), (), 1.5),
+        (task_d_hidden_sum, (), (14,), 0.3),
+        (task_grad_up, (), (), 1.0),
+        (task_norm_one_back, (), (43, 44), 1.0),
+        (task_d_context, (), (15,), 0.7),
+        (task_grad_out, (), (), 0.5),
+        (task_d_context_sum, (), (16,), 0.2),
     ]
-    tasks += [(functools.partial(task_attention_back, b, two), (), 1.0) for b, two in two_heads]
+    for two in range(3):
+        tasks += [(call(task_attention_back, b, two), (), (), 0.75) for b in range(2)]
+        tasks += [(call(task_grad_qkv, two), (), (), 0.4)]
     tasks += [
-        (task_grad_qkv, (), 1.2),
-        (task_token_grad, (), 1.0),
-        (task_sums, (), 0.8),
-        (task_sums_send, (), 0.8),
-        (task_token_grad_sum, (), 0.3),
+        (task_sums, (), (), 0.7),
+        (task_token_grad, (), (), 1.0),
+        (task_sums_send, (), (24,), 0.3),
+        (task_token_grad_sum, (), (17,), 0.3),
     ]
-    while tasks or plan.pending:
-        soonest = plan.pending[0][0] if plan.pending else None
-        ready = bool(tasks) and all(done[k] == PAIRS for k in tasks[0][1])
-        if plan.pending and (soonest <= plan.now or not ready):
-            plan.now = max(plan.now, soonest)
+    late, credit = [], 0
+    while tasks or plan.pending or plan.waiting or late:
+        plan.pump()
+        while plan.pending and plan.pending[0][0] <= plan.now and not plan.pending[0][2][0]:
             key = heapq.heappop(plan.pending)[2]
-            if key[0]:
-                plan.now += 0.1
-                on_gather(*key[1:])
+            if key[0] is None:
+                plan.here.add(key[1])
             else:
-                plan.now += 0.3
-                on_scatter(*key[1:])
+                late.append(key)
+        ready = bool(tasks) and (
+            all(done[k] == PIECES[k] for k in tasks[0][1]) and plan.here.issuperset(tasks[0][2])
+        )
+        if plan.pending and plan.pending[0][2][0] and plan.pending[0][0] <= plan.now:
+            plan.now += 0.1
+            on_gather(*heapq.heappop(plan.pending)[2][1:])
+        elif late and (not ready or credit > 0):
+            credit -= 1
+            on_scatter(*late.pop(0)[1:])
+        elif ready:
+            task, _, _, cost = tasks.pop(0)
+            plan.now += cost
+            credit = ADDS_BETWEEN
+            task()
+        elif plan.pending:
+            plan.now = max(plan.now, plan.pending[0][0])
         else:
-            task, _, cost = tasks.pop(0)
-            plan.now += cost
-            task()
-    for i in range(18, 24):
-        sib[i].wait_recv()
+            plan.now += 0.5
+    for k, parts in ((3, (18 + DOWN,)), (2, (22, 27, 28)), (1, (18 + OUT,)), (0, (18, 19, 20))):
+        for i in parts:
+            arrived(i)
+        if k == 2:
+            for j in range(8):
+                R.g[2][:, 2 * j * 192 : 2 * (j + 1) * 192] = jnp.concatenate(
+                    [R.mixed[:, x * hhalf + j * 192 : x * hhalf + (j + 1) * 192] for x in (0, 1)],
+                    axis=1,
+                )
+        if k == 0:
+            for c in range(2):
+                for two in range(3):
+                    for p in range(3):
+                        to = p * width + c * half + two * 128
+                        at = (3 * c + two) * 384 + p * 128
+                        R.g[0][:, to : to + 128] = R.mixed_qkv[:, at : at + 128]
+        stores[3 + k].start()
+    for store in stores:
+        store.wait()
     for copy in sent:
         copy.wait_send()
+
+
+def deliver_kernel(*refs):
+    found, given, near = refs[:OUTPUTS], refs[OUTPUTS : 2 * OUTPUTS + 8], refs[2 * OUTPUTS + 8 :]
+    singles, (in_sem, out_sem) = near[OUTPUTS:-2], near[-2:]
+    loads = [pltpu.make_async_copy(f, n, in_sem.at[i]) for i, (f, n) in enumerate(zip(found, near))]
+    for load in loads:
+        load.start()
+    stores = []
+
+    def store(src, dst):
+        copy = pltpu.make_async_copy(src, dst, out_sem.at[len(stores)])
+        copy.start()
+        stores.append(copy)
+
+    loads[2].wait()
+    for j, single in enumerate(singles):
+        single[...] = near[2][j : j + 1, 0 : single.shape[1]]
+        store(single, given[OUTPUTS - 1 + j])
+    for i in (0, 4, 3, 1, 5, 6):
+        loads[i].wait()
+        store(near[i], given[i - (i > 2)])
+    for copy in stores:
+        copy.wait()
 
 
 def fused(tokens, doc_ids, pad_mask, matrices, vectors, cotangent):
@@ -816,24 +1052,24 @@
     fl = jnp.float32
     lists, named = scratch_of(rows, width, hidden)
     operands = (
-        [tokens, doc_ids[None], pad_mask[None]]
+        [tokens, doc_ids[None], pad_mask[None], cotangent]
         + list(matrices)
         + [v[None] for v in vectors]
-        + [cotangent]
-    )
-    vmem = pl.BlockSpec(memory_space=pltpu.VMEM)
+    )
+    results = [
+        jax.ShapeDtypeStruct(tokens.shape, jnp.bfloat16),
+        jax.ShapeDtypeStruct(tokens.shape, fl),
+        jax.ShapeDtypeStruct((16, 128), fl),
+    ] + [jax.ShapeDtypeStruct(m.shape, fl) for m in matrices]
+    far = pl.BlockSpec(memory_space=pl.ANY)
     dma = pltpu.SemaphoreType.DMA
-    layer_out, token_grad, g0, g1, g2, g3, gv = pl.pallas_call(
+    found = pl.pallas_call(
         functools.partial(layer_kernel, tuple(named)),
-        out_shape=[
-            jax.ShapeDtypeStruct(tokens.shape, jnp.bfloat16),
-            jax.ShapeDtypeStruct(tokens.shape, fl),
-        ]
-        + [jax.ShapeDtypeStruct(m.shape, fl) for m in matrices]
-        + [jax.ShapeDtypeStruct((16, 128), fl)],
-        in_specs=[vmem] * len(operands),
-        out_specs=[vmem] * 7,
-        scratch_shapes=[pltpu.VMEM(shape, kind) for shape, kind in lists + list(named.values())]
+        out_shape=results,
+        in_specs=[far] * INPUTS,
+        out_specs=[far] * OUTPUTS,
+        scratch_shapes=[pltpu.VMEM(a.shape, a.dtype) for a in operands + results]
+        + [pltpu.VMEM(shape, kind) for shape, kind in lists + list(named.values())]
         + [
             dma((SIBLING_COPIES,)),
             dma((SIBLING_COPIES,)),
@@ -841,13 +1077,27 @@
             dma((COUNT, PAIRS)),
             dma((COUNT, PAIRS)),
             dma((COUNT, PAIRS)),
+            dma((INPUTS,)),
+            dma((OUTPUTS,)),
         ],
         compiler_params=pltpu.CompilerParams(
             collective_id=0, has_side_effects=True, vmem_limit_bytes=FUSED_VMEM
         ),
         name="layer",
     )(*operands)
-    s = [gv[j, : v.shape[0]] for j, v in enumerate(vectors)]
+    singles = [jax.ShapeDtypeStruct((1, v.shape[0]), fl) for v in vectors]
+    large = [r for i, r in enumerate(results) if i != 2]
+    given = pl.pallas_call(
+        deliver_kernel,
+        out_shape=large + singles,
+        in_specs=[far] * OUTPUTS,
+        out_specs=[far] * (len(large) + len(singles)),
+        scratch_shapes=[pltpu.VMEM(a.shape, a.dtype) for a in results + singles]
+        + [dma((OUTPUTS,)), dma((OUTPUTS + len(singles),))],
+        name="deliver",
+    )(*found)
+    layer_out, token_grad, g0, g1, g2, g3 = given[: len(large)]
+    s = [v[0] for v in given[len(large) :]]
     return (
         layer_out,
         token_grad,

time: 160 us -> 124 us (0.78)
  Pallas kernels: 150 us -> 123 us
  local copies, waits for them, and re-layouts: 8.77 us -> 0 us
    pallas_call x1 -> x2, Pallas kernels: 150 us -> 123 us  [the longest x1 121 us: fused(): pl.pallas_call(functools.partial(layer_kernel, tuple(named)), out_shape=r...]
    unnamed x16 -> x0, local copies, waits for them, and re-layouts: 6.02 us -> none
    squeeze x2 -> x0, local copies, waits for them, and re-layouts: 2.75 us -> none  [fused(): s = [gv[j, :v.shape[0]] for j, v in enumerate(vectors)]]
where the time goes in v2:
time: 124 us
  Pallas kernels  123 us (99%)
    pallas_call x1, Pallas kernels, fused(): pl.pallas_call(functools.partial(layer_kernel, tuple(named)), out_shape=r...  121 us

profile of v2, /device:TPU:1, one launch (start us, length us, event | category | flops | bytes accessed | tf_op | source)
XLA Modules:
  0.0 124.0 jit_solution(10788852326305566053)
XLA Ops:
  0.7 120.7 %layer.1 = (bf16[128,768]{1,0:T(8,128)(2,1)}, f32[128,768]{1,0:T(8,128)}, f32[16,128]{1,0:T(8,128)}, f32[24,2304]{1,0:T(8,128)}, f32[24,768]{1,0:T(8,128)}, /*index=5*/f32[24,3072]{1,0:T(8,128)}, f32[96,768]{1,0:T(8,128)}) custom-call(bf16[128,768]{1,0:T(8,128)(2,1)} %refs_0_.1, s32[1,128]{1,0:T(1,128)} %bitcast.20, s32[1,128]{1,0:T(1,128)} %bitcast.21, ...), custom_call_target="tpu_custom_call" | custom-call | tf_op jit(solution)/shard_map/layer/pallas_call | solution.py:1066
  121.4 2.4 %deliver.1 = (bf16[128,768]{1,0:T(8,128)(2,1)}, f32[128,768]{1,0:T(8,128)}, f32[24,2304]{1,0:T(8,128)}, f32[24,768]{1,0:T(8,128)}, f32[24,3072]{1,0:T(8,128)}, /...) custom-call(bf16[128,768]{1,0:T(8,128)(2,1)} %get-tuple-element.37.r, ...), custom_call_target="tpu_custom_call" | custom-call | tf_op jit(solution)/shard_map/deliver/pallas_call | solution.py:1090

commit v3 on v2

--- a/solution.py
+++ b/solution.py
@@ -118,37 +118,46 @@
 
 X, Y, Z1, Z2 = 0, 1, 2, 3
 GATHER_ORDERS = (
+    (Z2, Z1, X, Y),
     (Z2, Z1, Y, X),
-    (Z2, Z1, X, Y),
     (Y, Z2, Z1, X),
     (Z2, Z1, Y, X),
     (Z2, Z1, Y),
     (Z2, Z1, Y),
-    (Z2, Z1, Y, X),
+    (Z2, Z1, Y),
+    (Y, Z2, Z1),
+    (Y, Z2, Z1, X),
 )
 SCATTER_ORDERS = (
     (X, Z1, Z2, Y),
     (Y, X, Z1, Z2),
-    (X, Y, Z1, Z2),
-    (X, Y, Z1, Z2),
+    (Y, X, Z1, Z2),
+    (Y, X, Z1, Z2),
     (Y, Z1, Z2),
     (Y, Z1, Z2),
-    (Y, Z1, Z2, X),
+    (Y, Z1, Z2),
+    (Z1, Z2, Y),
+    (X, Z1, Z2, Y),
 )
-GATHER_FIRST = (0, 0, 2, 2, 4, 5, 0)
-SCATTER_FIRST = (3, 0, 2, 1, 2, 3, 2)
-ADDS_BETWEEN = 2
-ADD_US = (0.15, 0.15, 0.15, 0.15, 0.3, 0.3, 0.08)
+GATHER_FIRST = (0, 1, 2, 3, 4, 4, 5, 5, 0)
+SCATTER_FIRST = (3, 0, 0, 1, 1, 2, 3, 2, 3)
+ADDS_BETWEEN = 1
+ADD_US = (0.225, 0.225, 0.225, 0.225, 0.3, 0.3, 0.3, 0.3, 0.12)
 PAIRS = 16
-PIECES = (16, 16, 16, 16, 8, 8, 16)
-PIECE_ROWS = (48, 48, 48, 48, 96, 192, 32)
-PIECE_COLS = (384, 384, 384, 384, 768, 384, 128)
+PIECES = (16, 16, 16, 16, 8, 8, 8, 8, 16)
+PIECE_ROWS = (48, 48, 48, 48, 96, 96, 96, 96, 32)
+PIECE_COLS = (384, 384, 384, 384, 384, 384, 384, 384, 128)
+TRAVELLERS = 9
+BUFFER = (0, 1, 2, 3, 4, 4, 5, 5, 6)
+PLACE_ROWS = (48, 48, 48, 48, 96, 192, 32)
+PLACE_COLS = (384, 384, 384, 384, 768, 384, 128)
+PLACES = (16, 16, 16, 16, 8, 8, 16)
 OUT, UP, DOWN, VEC = 3, 4, 5, 6
 QUAD = 4
 COUNT = 7
 HOPS = {X: ((0, 1),), Y: ((1, 1),), Z1: ((2, 1),), Z2: ((2, 1), (3, 2))}
-LINK_BYTES_PER_US = 46e3
-HOP_US = 1.0
+LINK_BYTES_PER_US = 44e3
+HOP_US = 1.5
 CORE_BYTES_PER_US = 600e3
 BACKLOG_US = 1.5
 FUSED_VMEM = 58 * 1024 * 1024
@@ -212,8 +221,8 @@
 
 def stage_shape(k):
     if k == UP:
-        return ((QUAD, 32, PIECE_COLS[k]), jnp.bfloat16)
-    return (((PIECE_ROWS[k] // 2 + 15) // 16 * 16, PIECE_COLS[k]), jnp.bfloat16)
+        return ((QUAD, 32, PLACE_COLS[k]), jnp.bfloat16)
+    return (((PLACE_ROWS[k] // 2 + 15) // 16 * 16, PLACE_COLS[k]), jnp.bfloat16)
 
 
 def scratch_of(rows, width, hidden):
@@ -222,17 +231,17 @@
     hhalf, hquarter = hidden // 2, hidden // 4
     lists = []
     for shape_of in (
-        lambda k: ((PIECES[k] * PIECE_ROWS[k], PIECE_COLS[k]), bf),
-        lambda k: ((PIECES[k] * PIECE_ROWS[k], PIECE_COLS[k]), bf),
-        lambda k: ((PIECES[k] - 1, PIECE_ROWS[k], PIECE_COLS[k]), bf),
+        lambda k: ((PLACES[k] * PLACE_ROWS[k], PLACE_COLS[k]), bf),
+        lambda k: ((PLACES[k] * PLACE_ROWS[k], PLACE_COLS[k]), bf),
         stage_shape,
         stage_shape,
-        lambda k: ((PIECE_ROWS[k], PIECE_COLS[k]), fl),
+        lambda k: ((PLACE_ROWS[k], PLACE_COLS[k]), fl),
     ):
         lists += [shape_of(k) for k in range(COUNT)]
+    lists += [((PIECES[k] - 1, PIECE_ROWS[k], PIECE_COLS[k]), bf) for k in range(TRAVELLERS)]
     named = dict(
-        peer_vec=((PAIRS * PIECE_ROWS[VEC], PIECE_COLS[VEC]), bf),
-        stage_vec=((PAIRS * PIECE_ROWS[VEC], PIECE_COLS[VEC]), bf),
+        peer_vec=((PAIRS * PLACE_ROWS[VEC], PLACE_COLS[VEC]), bf),
+        stage_vec=((PAIRS * PLACE_ROWS[VEC], PLACE_COLS[VEC]), bf),
         tok=((both, width), bf),
         marks=((2, 8, rows), fl),
         vec32=((PAIRS * 32, 128), fl),
@@ -241,9 +250,8 @@
         qkv=((both, 3 * half), bf),
         probs=((HEADS, rows, rows), fl),
         ctx=((both, width), bf),
-        proj_s=((rows, half), fl),
+        proj_s=((both, half), fl),
         proj_r=((rows, half), fl),
-        proj_o=((rows, half), fl),
         hid=((rows, width), fl),
         n1=((rows, width), fl),
         i1=((rows, 128), fl),
@@ -273,9 +281,8 @@
         dctx_o=((both, half), fl),
         dctx=((both, half), bf),
         dqkv=((both, 3 * half), bf),
-        tg_s=((rows, width), fl),
+        tg_s=((both, width), fl),
         tg_r=((rows, width), fl),
-        tg_o=((rows, width), fl),
         sums=((16, width), fl),
         upsum=((8, hquarter), fl),
         mixed=((width // GROUP, hidden), fl),
@@ -297,7 +304,8 @@
     R.w, R.v = near_in[4:8], near_in[8:]
     R.layer_out, R.token_grad, R.gv = near_out[:3]
     R.g = near_out[3:]
-    R.whole, R.part, R.land, R.stage, R.peer, R.fin = (take(COUNT) for _ in range(6))
+    R.whole, R.part, R.stage, R.peer, R.fin = (take(COUNT) for _ in range(5))
+    R.land = take(TRAVELLERS)
     vars(R).update(zip(names, take(len(names))))
     sib_send, sib_recv, g_send, g_recv, s_send, s_recv, in_sem, out_sem = refs
     loads = [
@@ -399,7 +407,7 @@
                 for p in range(3)
             ]
             return jnp.concatenate([c.astype(fl) for c in cols], axis=1)
-        cols = PIECE_COLS[k]
+        cols = PLACE_COLS[k]
         ref = R.w[1] if k == OUT else R.w[3]
         return ref[:, pl.ds(by_core(cols, None if mine else 1), cols)].astype(fl)
 
@@ -446,20 +454,29 @@
     R.tok[own_rows, :] = R.tokens[...]
 
     plan.now = 3.0
-    piece_bytes = [2 * PIECE_ROWS[k] * PIECE_COLS[k] for k in range(COUNT)]
-    done = [1] * COUNT
-
-    def piece_at(k, r):
-        n = PIECE_ROWS[k]
-        place = pair_of(r) if PIECES[k] == PAIRS else quad_of(r)
-        return pl.ds(pl.multiple_of(place * n, n), n)
+    piece_bytes = [2 * PIECE_ROWS[k] * PIECE_COLS[k] for k in range(TRAVELLERS)]
+    done = [1] * TRAVELLERS
+
+    def place_at(k, r):
+        n = PLACE_ROWS[k]
+        place = pair_of(r) if PLACES[k] == PAIRS else quad_of(r)
+        return pl.multiple_of(place * n, n)
+
+    def piece_of(refs, k, r):
+        to = BUFFER[k]
+        row, col = place_at(to, r), 0
+        if k > 0 and BUFFER[k - 1] == to:
+            if to == UP:
+                col = PIECE_COLS[k]
+            else:
+                row = pl.multiple_of(row + PIECE_ROWS[k], PIECE_ROWS[k])
+        return refs[to].at[pl.ds(row, PIECE_ROWS[k]), pl.ds(col, PIECE_COLS[k])]
 
     def gather_move(k, r, b):
-        at = piece_at(k, r)
         slot = r | (1 << b)
         copy = pltpu.make_async_remote_copy(
-            src_ref=R.whole[k].at[at],
-            dst_ref=R.whole[k].at[at],
+            src_ref=piece_of(R.whole, k, r),
+            dst_ref=piece_of(R.whole, k, r),
             send_sem=g_send.at[k, slot],
             recv_sem=g_recv.at[k, slot],
             device_id=(device_along(b),),
@@ -479,13 +496,17 @@
             mine = R.vec32[pl.ds(0, 16), :] if k == VEC else shard_half(k, True)
             theirs = R.peer[k][...].astype(fl)[: mine.shape[0]]
             rows_in = [jnp.where(is_first, mine, theirs), jnp.where(is_first, theirs, mine)]
-        R.whole[k][piece_at(k, 0), :] = jnp.concatenate(rows_in, axis=0).astype(bf)
-        for b in GATHER_ORDERS[k]:
-            gather_move(k, 0, b)
+        R.whole[k][pl.ds(place_at(k, 0), PLACE_ROWS[k]), :] = jnp.concatenate(
+            rows_in, axis=0
+        ).astype(bf)
+        for j in range(TRAVELLERS):
+            if BUFFER[j] == k:
+                for b in GATHER_ORDERS[j]:
+                    gather_move(j, 0, b)
         plan.pump()
 
     def on_gather(k, r, b):
-        here = R.whole[k].at[piece_at(k, r)]
+        here = piece_of(R.whole, k, r)
         pltpu.make_async_remote_copy(
             src_ref=here,
             dst_ref=here,
@@ -500,7 +521,7 @@
         done[k] += 1
 
     slot_of = []
-    for k in range(COUNT):
+    for k in range(TRAVELLERS):
         table = {}
         for step in range(len(SCATTER_ORDERS[k])):
             for r in subsets(SCATTER_ORDERS[k], step):
@@ -510,7 +531,7 @@
 
     def held(k, step, r):
         if step < 0:
-            return R.part[k].at[piece_at(k, r)]
+            return piece_of(R.part, k, r)
         return R.land[k].at[slot_of[k][step, r]]
 
     def scatter_move(k, step, r):
@@ -541,7 +562,7 @@
             return
         if k == UP:
             at = pl.ds(pl.multiple_of(x_at * hhalf + core * hquarter, 128), hquarter)
-            n = PIECE_ROWS[UP] // QUAD
+            n = PLACE_ROWS[UP] // QUAD
 
             def share(q):
                 return R.fin[UP].at[pl.ds(pl.multiple_of(q * n, n), n)]
@@ -554,7 +575,7 @@
                 to_sibling(i, share(q), R.mixed.at[:, at], device)
             R.mixed[:, at] = share(member)[...]
             return
-        n = PIECE_ROWS[k] // 2
+        n = PLACE_ROWS[k] // 2
         mine = R.fin[k].at[pl.ds(by_core(n), n)]
         theirs = R.fin[k].at[pl.ds(by_core(n, 1), n)]
         if k < 3:
@@ -564,6 +585,7 @@
         to_sibling(18 + k, theirs, into.at[:, at])
         into[:, at] = mine[...]
 
+    unfinished = [BUFFER.count(k) for k in range(COUNT)]
     summed = set()
     early = {}
 
@@ -581,12 +603,19 @@
         copies[k, step, r].wait_recv()
         order = SCATTER_ORDERS[k]
         before, now = held(k, step - 1, r), held(k, step, r)
-        total = now[...].astype(fl) + before[...].astype(fl)
         if step == len(order) - 1:
-            R.fin[k][...] = total
-            finish(k)
+            to = BUFFER[k]
+            row, col = 0, 0
+            if k > 0 and BUFFER[k - 1] == to:
+                row, col = (0, PIECE_COLS[k]) if to == UP else (PIECE_ROWS[k], 0)
+            R.fin[to][row : row + PIECE_ROWS[k], col : col + PIECE_COLS[k]] = now[...].astype(
+                fl
+            ) + before[...].astype(fl)
+            unfinished[to] -= 1
+            if not unfinished[to]:
+                finish(to)
             return
-        now[...] = total.astype(bf)
+        now[...] = now[...] + before[...]
         if r >> order[step + 1] & 1:
             scatter_move(k, step + 1, r)
 
@@ -679,9 +708,8 @@
         arrived(7)
         arrived(45)
         arrived(46)
-        R.proj_s[...] = dot(R.ctx[sib_rows, :], R.whole[OUT][...])
-        to_sibling(8, R.proj_s, R.proj_r)
-        R.proj_o[...] = dot(R.ctx[own_rows, :], R.whole[OUT][...])
+        R.proj_s[...] = dot(R.ctx[...], R.whole[OUT][...])
+        to_sibling(8, R.proj_s.at[sib_rows], R.proj_r)
 
     def norm(values):
         centred = values - jnp.mean(values, axis=-1, keepdims=True)
@@ -692,7 +720,7 @@
         arrived(8)
         attn = (
             R.tokens[...].astype(fl)
-            + side_by_side(R.proj_o[...], R.proj_r[...])
+            + side_by_side(R.proj_s[own_rows, :], R.proj_r[...])
             + vec(2)
         )
         normed, inverse = norm(attn)
@@ -743,17 +771,23 @@
     def task_ffn():
         arrived(33)
         arrived(34)
-        for i, other_core in ((35, 1), (36, 0)):
-            at = pl.ds(by_core(rows, 1 if other_core else None), rows)
-            R.ffn_xs[at, :] = dot(R.act[quad_rows(1, other_core), :], R.whole[DOWN][...]).astype(bf)
-            to_sibling(i, R.ffn_xs.at[at], R.ffn_xr.at[at], across)
+        R.ffn_xs[...] = dot(R.act[chip_rows(1), :], R.whole[DOWN][...]).astype(bf)
+        for part, ids in ((0, (35, 36)), (1, (47, 48))):
+            for i, other_core in zip(ids, (1, 0)):
+                at = local_rows(other_core, part)
+                to_sibling(i, R.ffn_xs.at[at], R.ffn_xr.at[at], across)
         R.ffn_o[...] = dot(R.act[chip_rows(0), :], R.whole[DOWN][...])
 
-    def task_ffn_sum():
-        arrived(35)
-        R.ffn_s[...] = R.ffn_o[sib_rows, :] + R.ffn_xr[sib_rows, :].astype(fl)
-        to_sibling(11, R.ffn_s, R.ffn_r)
-        arrived(36)
+    def local_rows(other_core, part):
+        at = (1 - core if other_core else core) * rows + part * (rows // 2)
+        return pl.ds(pl.multiple_of(at, 64), rows // 2)
+
+    def task_ffn_sum(part):
+        arrived((35, 47)[part])
+        at, to = local_rows(1, part), pl.ds(part * (rows // 2), rows // 2)
+        R.ffn_s[to, :] = R.ffn_o[at, :] + R.ffn_xr[at, :].astype(fl)
+        to_sibling((11, 49)[part], R.ffn_s.at[to], R.ffn_r.at[to])
+        arrived((36, 48)[part])
 
     def back_of_norm(upstream, normed, inverse, gain):
         scaled = upstream * gain
@@ -763,39 +797,51 @@
             - normed * jnp.mean(scaled * normed, axis=-1, keepdims=True)
         )
 
-    def add_sum(j, values):
-        R.sums[j : j + 1, :] = jnp.sum(values, axis=0, keepdims=True)
-
-    def task_norm_two():
-        arrived(11)
-        mine = R.ffn_o[own_rows, :] + R.ffn_xr[own_rows, :].astype(fl)
-        total = R.hid[...] + side_by_side(mine, R.ffn_r[...]) + vec(5)
+    def add_sum(j, values, more=False):
+        total = jnp.sum(values, axis=0, keepdims=True)
+        R.sums[j : j + 1, :] = R.sums[j : j + 1, :] + total if more else total
+
+    def task_norm_two(part):
+        arrived((11, 49)[part])
+        at, to = local_rows(0, part), pl.ds(part * (rows // 2), rows // 2)
+        mine = R.ffn_o[at, :] + R.ffn_xr[at, :].astype(fl)
+        total = R.hid[to, :] + side_by_side(mine, R.ffn_r[to, :]) + vec(5)
         normed, inverse = norm(total)
-        R.layer_out[...] = (normed * vec(6) + vec(7)).astype(bf)
-        stores[0].start()
-        upstream = R.cotangent[...].astype(fl)
+        R.layer_out[to, :] = (normed * vec(6) + vec(7)).astype(bf)
+        upstream = R.cotangent[to, :].astype(fl)
         d_ffn = back_of_norm(upstream, normed, inverse, vec(6))
-        R.dff[...] = d_ffn
-        R.dfb[quad_rows(0, 0), :] = d_ffn.astype(bf)
-        spread_rows(R.dfb, 12, 37)
-        add_sum(6, upstream * normed)
-        add_sum(7, upstream)
-        add_sum(5, d_ffn)
+        R.dff[to, :] = d_ffn
+        rows_at = quad_rows(0, 0, rows // 2, part * (rows // 2))
+        R.dfb[rows_at, :] = d_ffn.astype(bf)
+        to_sibling(37 + part, R.dfb.at[rows_at], R.dfb.at[rows_at], across)
+        add_sum(6, upstream * normed, part)
+        add_sum(7, upstream, part)
+        add_sum(5, d_ffn, part)
+        if part:
+            stores[0].start()
+            rows_at = quad_rows(0, 0)
+            to_sibling(12, R.dfb.at[rows_at], R.dfb.at[rows_at])
+
+    def pass_half(ref, first, part):
+        arrived(first + part)
+        at = quad_rows(1, 0, rows // 2, part * (rows // 2))
+        to_sibling(first + 2 + part, ref.at[at], ref.at[at])
 
     def task_grad_down():
-        arrived(39)
-        arrived(40)
-
         def body(t, carry):
             at = pl.ds(pl.multiple_of(t * tile, tile), tile)
             R.part[DOWN][at, :] = dot(R.act[:, at], R.dfb[:, own_half], ROWS_BOTH).astype(bf)
             return carry
 
         lax.fori_loop(0, hhalf // tile, body, 0)
-        scatter_start(DOWN)
+        scatter_start(6)
+        scatter_start(7)
 
     def task_d_act(other):
-        if not other:
+        if other:
+            arrived(39)
+            arrived(40)
+        else:
             arrived(12)
         at = chip_rows(other)
         right = R.dfb[at, own_half]
@@ -817,14 +863,15 @@
         lax.fori_loop(0, hquarter // tile, body, 0)
 
     def task_d_hidden():
-        for i, other_x in ((14, 1), (43, 0)):
-            at = pl.ds(other_x * rows, rows)
-            R.dhid_s[at, :] = dot(R.dpre[quad_rows(other_x, 1), :], R.whole[UP][...], COLS_BOTH)
-            to_sibling(i, R.dhid_s.at[at], R.dhid_r.at[at])
-        for other_x in (1, 0):
-            R.dhid_o[pl.ds(other_x * rows, rows), :] = dot(
-                R.dpre[quad_rows(other_x, 0), :], R.whole[UP][...], COLS_BOTH
+        for other_core, into in ((1, R.dhid_s), (0, R.dhid_o)):
+            left = jnp.concatenate(
+                [R.dpre[quad_rows(other_x, other_core), :] for other_x in (0, 1)], axis=0
             )
+            into[...] = dot(left, R.whole[UP][...], COLS_BOTH)
+            if other_core:
+                for i, other_x in ((14, 1), (43, 0)):
+                    at = pl.ds(other_x * rows, rows)
+                    to_sibling(i, R.dhid_s.at[at], R.dhid_r.at[at])
 
     def task_d_hidden_sum():
         arrived(14)
@@ -833,13 +880,10 @@
         to_sibling(44, R.dhid_xs, R.dhid_xr, across)
 
     def task_grad_up():
-        def body(t, carry):
-            at = pl.ds(pl.multiple_of(t * tile, tile), tile)
+        for t in range(2):
+            at = pl.ds(t * tile, tile)
             R.part[UP][:, at] = dot(R.hb[...], R.dpre[:, at], ROWS_BOTH).astype(bf)
-            return carry
-
-        lax.fori_loop(0, hquarter // tile, body, 0)
-        scatter_start(UP)
+            scatter_start(4 + t)
 
     def task_norm_one_back():
         arrived(43)
@@ -904,16 +948,12 @@
         R.part[two][...] = dot(R.tok[...], R.dqkv[:, at], ROWS_BOTH).astype(bf)
         scatter_start(two)
 
-    def through_qkv(at):
-        return sum(
-            dot(R.dqkv[at, pl.ds(two * 384, 384)], R.whole[two][...], COLS_BOTH)
+    def task_token_grad():
+        R.tg_s[...] = sum(
+            dot(R.dqkv[:, pl.ds(two * 384, 384)], R.whole[two][...], COLS_BOTH)
             for two in range(3)
         )
-
-    def task_token_grad():
-        R.tg_s[...] = through_qkv(sib_rows)
-        to_sibling(17, R.tg_s, R.tg_r)
-        R.tg_o[...] = R.dat[...] + through_qkv(own_rows)
+        to_sibling(17, R.tg_s.at[sib_rows], R.tg_r)
 
     def task_sums():
         chosen, owner = pick(width, small), owner_is(width, small)
@@ -929,31 +969,34 @@
     def task_sums_send():
         arrived(24)
         R.part[VEC][...] = (R.vec32[...] + R.peer_vec[...].astype(fl)).astype(bf)
-        scatter_start(VEC)
+        scatter_start(8)
 
     def task_token_grad_sum():
         arrived(17)
-        R.token_grad[...] = R.tg_o[...] + R.tg_r[...]
+        R.token_grad[...] = R.dat[...] + R.tg_s[own_rows, :] + R.tg_r[...]
         stores[1].start()
 
     call = functools.partial
-    tasks = [(task_clear_sums, (), (), 0.1), (task_vectors, (VEC,), (), 0.6)]
+    tasks = [(task_clear_sums, (), (), 0.1), (task_vectors, (8,), (), 0.6)]
     for two in range(3):
         tasks += [(call(task_qkv, two), (two,), (5, 6), 0.4)]
         tasks += [(call(task_attention, b, two), (), (), 0.9) for b in range(2)]
     tasks += [
         (task_project, (OUT,), (7, 45, 46), 1.0),
         (task_norm_one, (), (8,), 1.0),
-        (call(task_up, 0), (UP,), (9,), 1.8),
+        (call(task_up, 0), (4, 5), (9,), 1.8),
         (call(pass_on, R.hb, 29), (), (29, 30), 0.2),
         (call(task_up, 1), (), (31, 32), 1.8),
-        (task_ffn, (DOWN,), (33, 34), 1.5),
-        (task_ffn_sum, (), (35, 36), 0.4),
-        (task_norm_two, (), (11,), 1.2),
+        (task_ffn, (6, 7), (33, 34), 1.5),
+        (call(task_ffn_sum, 0), (), (35, 36), 0.2),
+        (call(task_norm_two, 0), (), (11,), 0.7),
+        (call(task_ffn_sum, 1), (), (47, 48), 0.2),
+        (call(task_norm_two, 1), (), (49,), 0.7),
         (call(task_d_act, 0), (), (12,), 1.2),
-        (call(pass_on, R.dfb, 37), (), (37, 38), 0.2),
-        (task_grad_down, (), (39, 40), 1.7),
-        (call(task_d_act, 1), (), (), 1.2),
+        (call(pass_half, R.dfb, 37, 0), (), (37,), 0.1),
+        (call(pass_half, R.dfb, 37, 1), (), (38,), 0.1),
+        (call(task_d_act, 1), (), (39, 40), 1.2),
+        (task_grad_down, (), (), 1.7),
         (task_d_pre, (), (41, 42), 0.6),
         (task_d_hidden, (), (), 1.5),
         (task_d_hidden_sum, (), (14,), 0.3),
@@ -1073,10 +1116,10 @@
         + [
             dma((SIBLING_COPIES,)),
             dma((SIBLING_COPIES,)),
-            dma((COUNT, PAIRS)),
-            dma((COUNT, PAIRS)),
-            dma((COUNT, PAIRS)),
-            dma((COUNT, PAIRS)),
+            dma((TRAVELLERS, PAIRS)),
+            dma((TRAVELLERS, PAIRS)),
+            dma((TRAVELLERS, PAIRS)),
+            dma((TRAVELLERS, PAIRS)),
             dma((INPUTS,)),
             dma((OUTPUTS,)),
         ],

time: 124 us -> 120 us (0.968)
  Pallas kernels: 123 us -> 119 us
    pallas_call x1, Pallas kernels: 121 us -> 117 us  [fused(): pl.pallas_call(functools.partial(layer_kernel, tuple(named)), out_shape=r...]
where the time goes in v3:
time: 120 us
  Pallas kernels  119 us (99%)
    pallas_call x1, Pallas kernels, fused(): pl.pallas_call(functools.partial(layer_kernel, tuple(named)), out_shape=r...  117 us
    pallas_call x1, Pallas kernels, fused(): pl.pallas_call(deliver_kernel, out_shape=large + singles, in_specs=[far]...  2.44 us

profile of v3, /device:TPU:1, one launch (start us, length us, event | category | flops | bytes accessed | tf_op | source)
XLA Modules:
  0.0 120.0 jit_solution(14602923678056920525)
XLA Ops:
  0.7 116.7 %layer.1 = (bf16[128,768]{1,0:T(8,128)(2,1)}, f32[128,768]{1,0:T(8,128)}, f32[16,128]{1,0:T(8,128)}, f32[24,2304]{1,0:T(8,128)}, f32[24,768]{1,0:T(8,128)}, /*index=5*/f32[24,3072]{1,0:T(8,128)}, f32[96,768]{1,0:T(8,128)}) custom-call(bf16[128,768]{1,0:T(8,128)(2,1)} %refs_0_.1, s32[1,128]{1,0:T(1,128)} %bitcast.20, s32[1,128]{1,0:T(1,128)} %bitcast.21, ...), custom_call_target="tpu_custom_call" | custom-call | tf_op jit(solution)/shard_map/layer/pallas_call | solution.py:1109
  117.4 2.4 %deliver.1 = (bf16[128,768]{1,0:T(8,128)(2,1)}, f32[128,768]{1,0:T(8,128)}, f32[24,2304]{1,0:T(8,128)}, f32[24,768]{1,0:T(8,128)}, f32[24,3072]{1,0:T(8,128)}, /...) custom-call(bf16[128,768]{1,0:T(8,128)(2,1)} %get-tuple-element.37.r, ...), custom_call_target="tpu_custom_call" | custom-call | tf_op jit(solution)/shard_map/deliver/pallas_call | solution.py:1133

commit v4 on v3

--- a/solution.py
+++ b/solution.py
@@ -140,7 +140,7 @@
     (X, Z1, Z2, Y),
 )
 GATHER_FIRST = (0, 1, 2, 3, 4, 4, 5, 5, 0)
-SCATTER_FIRST = (3, 0, 0, 1, 1, 2, 3, 2, 3)
+SCATTER_FIRST = (3, 0, 0, 1, 1, 2, 3, 1, 3)
 ADDS_BETWEEN = 1
 ADD_US = (0.225, 0.225, 0.225, 0.225, 0.3, 0.3, 0.3, 0.3, 0.12)
 PAIRS = 16
@@ -976,6 +976,24 @@
         R.token_grad[...] = R.dat[...] + R.tg_s[own_rows, :] + R.tg_r[...]
         stores[1].start()
 
+    def task_store_down():
+        arrived(18 + DOWN)
+        stores[6].start()
+
+    def task_store_out():
+        arrived(18 + OUT)
+        stores[4].start()
+
+    def task_store_up():
+        for i in (22, 27, 28):
+            arrived(i)
+        for j in range(8):
+            R.g[2][:, 2 * j * 192 : 2 * (j + 1) * 192] = jnp.concatenate(
+                [R.mixed[:, x * hhalf + j * 192 : x * hhalf + (j + 1) * 192] for x in (0, 1)],
+                axis=1,
+            )
+        stores[5].start()
+
     call = functools.partial
     tasks = [(task_clear_sums, (), (), 0.1), (task_vectors, (8,), (), 0.6)]
     for two in range(3):
@@ -999,8 +1017,8 @@
         (task_grad_down, (), (), 1.7),
         (task_d_pre, (), (41, 42), 0.6),
         (task_d_hidden, (), (), 1.5),
+        (task_grad_up, (), (), 1.0),
         (task_d_hidden_sum, (), (14,), 0.3),
-        (task_grad_up, (), (), 1.0),
         (task_norm_one_back, (), (43, 44), 1.0),
         (task_d_context, (), (15,), 0.7),
         (task_grad_out, (), (), 0.5),
@@ -1014,6 +1032,11 @@
         (task_token_grad, (), (), 1.0),
         (task_sums_send, (), (24,), 0.3),
         (task_token_grad_sum, (), (17,), 0.3),
+    ]
+    tasks += [
+        (task_store_down, (), (18 + DOWN,), 0.1),
+        (task_store_up, (), (22, 27, 28), 1.0),
+        (task_store_out, (), (18 + OUT,), 0.1),
     ]
     late, credit = [], 0
     while tasks or plan.pending or plan.waiting or late:
@@ -1042,23 +1065,15 @@
             plan.now = max(plan.now, plan.pending[0][0])
         else:
             plan.now += 0.5
-    for k, parts in ((3, (18 + DOWN,)), (2, (22, 27, 28)), (1, (18 + OUT,)), (0, (18, 19, 20))):
-        for i in parts:
-            arrived(i)
-        if k == 2:
-            for j in range(8):
-                R.g[2][:, 2 * j * 192 : 2 * (j + 1) * 192] = jnp.concatenate(
-                    [R.mixed[:, x * hhalf + j * 192 : x * hhalf + (j + 1) * 192] for x in (0, 1)],
-                    axis=1,
-                )
-        if k == 0:
-            for c in range(2):
-                for two in range(3):
-                    for p in range(3):
-                        to = p * width + c * half + two * 128
-                        at = (3 * c + two) * 384 + p * 128
-                        R.g[0][:, to : to + 128] = R.mixed_qkv[:, at : at + 128]
-        stores[3 + k].start()
+    for i in (18, 19, 20):
+        arrived(i)
+    for c in range(2):
+        for two in range(3):
+            for p in range(3):
+                to = p * width + c * half + two * 128
+                at = (3 * c + two) * 384 + p * 128
+                R.g[0][:, to : to + 128] = R.mixed_qkv[:, at : at + 128]
+    stores[3].start()
     for store in stores:
         store.wait()
     for copy in sent:

time: 120 us -> 120 us (level)
  no operation moved by 1% of the time
where the time goes in v4:
time: 120 us
  Pallas kernels  119 us (99%)
    pallas_call x1, Pallas kernels, fused(): pl.pallas_call(functools.partial(layer_kernel, tuple(named)), out_shape=r...  116 us
    pallas_call x1, Pallas kernels, fused(): pl.pallas_call(deliver_kernel, out_shape=large + singles, in_specs=[far]...  2.44 us

profile of v4, /device:TPU:1, one launch (start us, length us, event | category | flops | bytes accessed | tf_op | source)
XLA Modules:
  0.0 119.7 jit_solution(15007550981265167854)
XLA Ops:
  0.7 116.4 %layer.1 = (bf16[128,768]{1,0:T(8,128)(2,1)}, f32[128,768]{1,0:T(8,128)}, f32[16,128]{1,0:T(8,128)}, f32[24,2304]{1,0:T(8,128)}, f32[24,768]{1,0:T(8,128)}, /*index=5*/f32[24,3072]{1,0:T(8,128)}, f32[96,768]{1,0:T(8,128)}) custom-call(bf16[128,768]{1,0:T(8,128)(2,1)} %refs_0_.1, s32[1,128]{1,0:T(1,128)} %bitcast.20, s32[1,128]{1,0:T(1,128)} %bitcast.21, ...), custom_call_target="tpu_custom_call" | custom-call | tf_op jit(solution)/shard_map/layer/pallas_call | solution.py:1124
  117.1 2.4 %deliver.1 = (bf16[128,768]{1,0:T(8,128)(2,1)}, f32[128,768]{1,0:T(8,128)}, f32[24,2304]{1,0:T(8,128)}, f32[24,768]{1,0:T(8,128)}, f32[24,3072]{1,0:T(8,128)}, /...) custom-call(bf16[128,768]{1,0:T(8,128)(2,1)} %get-tuple-element.37.r, ...), custom_call_target="tpu_custom_call" | custom-call | tf_op jit(solution)/shard_map/deliver/pallas_call | solution.py:1148
